TPU v7x, 256 devices: a whole 4x4x8 slice. The times are simulated.
256 devices in a mesh: member: 32 (over y, z), patch: 4 (over x), level: 2 (over core).
Axes of the slice: x: 4, y: 4, z: 8, core: 2. Of those that a mesh axis runs over, the one named last changes fastest.
Arguments:
- ensemble: bfloat16 [256, 4, 32, 2, 12, 1024], P('member', 'patch', None, 'level'), may hold values from -6 to 6
- observations: float32 [4, 32, 2, 128], P('patch', 'member'), may hold values from -9 to 9
- precision: float32 [4, 32, 2, 128], P('patch', 'member'), may hold values from 0.25 to 4
- valid_count: int32 [4, 32, 2], P('patch', 'member'), may hold values from 16 to 128, as said below
- position: int32 [4, 32, 2, 128], P('patch', 'member'), may hold values from 0 to 12287
- level_kernel: float32 [2, 12], P('level'), may hold values from -4 to 4
- listed_blocks: int32 [4, 32, 8], P('patch', 'member'), may hold values from 0 to 17, as said below
Outputs:
- analysis: bfloat16 [256, 4, 32, 2, 12, 1024], P('member', 'patch', None, 'level')
Inputs may be any that keep to these rules, and one draw needn't show every extreme that they name: `valid_count`: the valid observations of a block are its first slots; some block is full and some holds 16. `listed_blocks`: the entries of one patch are distinct, include both of the patch's own blocks (candidates 8 and 9), and name only patches inside the grid.
All inputs are finite; a program needn't handle non-finite values.
Results may differ from a plain program's by a relative error of at most 0.0082.
Values may be sent and summed in bfloat16 or wider, within the bound.
No kernel may reach another device: no remote copies, remote signals or barrier semaphores. Data moves between devices by JAX's collectives and lax.ppermute only.
A program may use at most 128 MiB of HBM per device.

v0:
```python
import jax
import jax.numpy as jnp
from jax import lax
from jax.sharding import PartitionSpec as P

VARIABLES = 12
COLUMNS = 1024
SLOTS = 128
OWN_BLOCKS = 2
LISTED = 8
SWEEPS = 6


exact_precision = lax.Precision.HIGHEST


def extended(cells, sides, width):
    for axis, dim in sides:
        count = lax.axis_size(axis)
        ends = count - 1
        head = lax.slice_in_dim(cells, 0, width, axis=dim)
        tail = lax.slice_in_dim(cells, cells.shape[dim] - width, cells.shape[dim], axis=dim)
        cells = jnp.concatenate(
            [
                lax.ppermute(tail, axis, [(i, (i + 1) % count) for i in range(ends)]),
                cells,
                lax.ppermute(head, axis, [((i + 1) % count, i) for i in range(ends)]),
            ],
            axis=dim,
        )
    return cells


def taper_of(listed):
    stepped = listed // OWN_BLOCKS
    moved = jnp.abs(stepped // 3 - 1) + jnp.abs(stepped % 3 - 1)
    return jnp.where(moved == 0, 1.0, jnp.where(moved == 1, 0.6, 0.35)).astype(jnp.float32)


def weights_for(candidates, pairs, listed):
    members = candidates.shape[0]
    candidate_count = candidates.shape[1]
    choose_iota = lax.broadcasted_iota(jnp.int32, (LISTED, candidate_count), 1)
    selector = listed[:, None] == choose_iota
    chosen = jnp.einsum(
        "kjs,lj->kls", candidates, selector.astype(jnp.bfloat16), preferred_element_type=jnp.float32
    )
    chosen = chosen.astype(jnp.bfloat16).reshape(members, LISTED * SLOTS)
    picked = jnp.einsum(
        "ajs,lj->als", pairs, selector.astype(jnp.float32), precision=exact_precision
    )
    tapering = taper_of(listed)
    widened = lax.optimization_barrier(chosen).astype(jnp.float32)
    centre = jnp.mean(widened, axis=0)
    obs_pert = (widened - centre).astype(jnp.bfloat16)
    weight = (picked[1] * tapering[:, None]).reshape(LISTED * SLOTS)
    innovation = picked[0].reshape(LISTED * SLOTS) - centre
    pert_wide = lax.optimization_barrier(obs_pert).astype(jnp.float32)
    scaled = (pert_wide * jnp.sqrt(weight)).astype(jnp.bfloat16)
    identity = jnp.eye(members, dtype=jnp.float32)
    system = lax.dot_general(
        scaled, scaled, (((1,), (1,)), ((), ())), preferred_element_type=jnp.float32
    )
    system = system + (members - 1) / 1.1 * identity
    scaling = jnp.sqrt(jnp.sum(system * system))
    iterate = system / scaling
    inverse_root = identity
    for iteration in range(SWEEPS):
        middle = 1.5 * identity - 0.5 * jnp.dot(inverse_root, iterate, precision=exact_precision)
        iterate = jnp.dot(iterate, middle, precision=exact_precision)
        inverse_root = jnp.dot(middle, inverse_root, precision=exact_precision)
    forcing = jnp.dot(pert_wide, weight * innovation, precision=exact_precision)
    inner = jnp.dot(inverse_root, forcing, precision=exact_precision)
    mean_weight = jnp.dot(inverse_root, inner, precision=exact_precision) / scaling
    return (jnp.sqrt((members - 1) / scaling) * inverse_root + mean_weight[:, None]).astype(
        jnp.bfloat16
    )


def apply_weights(weights, fields):
    field_mean = jnp.mean(fields, axis=0, dtype=jnp.float32)
    field_pert = (fields - field_mean).astype(jnp.bfloat16)
    updated = lax.dot_general(
        weights, field_pert, (((0,), (0,)), ((), ())), preferred_element_type=jnp.float32
    )
    return (updated + field_mean).astype(jnp.bfloat16)


def observe(shaped_fields, where_flat, kernel):
    patch_count = where_flat.shape[0]
    slot_count = where_flat.shape[1]
    column_of = where_flat % COLUMNS
    variable_of = where_flat // COLUMNS
    column_iota = lax.broadcasted_iota(jnp.int32, (patch_count, COLUMNS, slot_count), 1)
    column_hot = (column_of[:, None, :] == column_iota).astype(jnp.bfloat16)
    spread = jnp.einsum(
        "kpvq,pqo->kpvo", shaped_fields, column_hot, preferred_element_type=jnp.float32
    )
    variable_iota = lax.broadcasted_iota(jnp.int32, (patch_count, VARIABLES, slot_count), 1)
    variable_weight = jnp.where(
        variable_of[:, None, :] == variable_iota, kernel[None, :, None], 0.0
    )
    return jnp.sum(spread * variable_weight[None], axis=2)


def body(ensemble, observations, precision, valid_count, position, level_kernel, listed_blocks):
    kernel = level_kernel[0]
    local_members = ensemble.shape[0]
    row_patches = ensemble.shape[2]
    where_all = lax.all_gather(position, "member", axis=1, tiled=True)
    shaped_fields = ensemble.reshape(local_members, row_patches, VARIABLES, COLUMNS)
    level_term = observe(shaped_fields, where_all.reshape(row_patches, OWN_BLOCKS * SLOTS), kernel)
    summed = lax.psum(level_term, "level")
    equiv_local = summed.astype(jnp.bfloat16).reshape(
        local_members, 1, row_patches, OWN_BLOCKS, SLOTS
    )
    fields, equivalent = (
        lax.all_to_all(ensemble, "member", split_axis=2, concat_axis=0, tiled=True),
        lax.all_to_all(equiv_local, "member", split_axis=2, concat_axis=0, tiled=True),
    )
    members = equivalent.shape[0]
    own_patches = equivalent.shape[2]
    slot_index = lax.broadcasted_iota(jnp.int32, precision.shape, 3)
    precision_used = jnp.where(slot_index < valid_count[..., None], precision, 0.0)
    observation_pair = jnp.stack([observations, precision_used])
    equiv_near = extended(equivalent, (("member", 2), ("patch", 1)), 1)
    pairs_near = extended(observation_pair, (("member", 2), ("patch", 1)), 1)
    fields_flat = fields.reshape(members, own_patches, VARIABLES * COLUMNS)
    patch_slot = 0
    candidates = equiv_near.reshape(members, 9 * OWN_BLOCKS, SLOTS)
    pairs = pairs_near.reshape(2, 9 * OWN_BLOCKS, SLOTS)
    weight_list = [weights_for(candidates, pairs, listed_blocks[0, patch_slot])]
    all_weights = jnp.stack(weight_list)
    patch_slot = 0
    results = [apply_weights(all_weights[patch_slot], fields_flat[:, patch_slot])]
    analysed = jnp.stack(results, axis=1).reshape(members, 1, own_patches, 1, VARIABLES, COLUMNS)
    return lax.all_to_all(analysed, "member", split_axis=0, concat_axis=2, tiled=True)


def solution(mesh):
    placed = (
        P("member", "patch", None, "level", None, None),
        P("patch", "member", None, None),
        P("patch", "member", None, None),
        P("patch", "member", None),
        P("patch", "member", None, None),
        P("level", None),
        P("patch", "member", None),
    )
    return jax.shard_map(
        body,
        mesh=mesh,
        in_specs=placed,
        out_specs=P("member", "patch", None, "level", None, None),
        check_vma=False,
    )
```

profile of v0, /device:TPU:6, one launch (start us, length us, event | category | flops | bytes accessed | tf_op | source)
XLA Modules:
  0.0 504.4 jit_solution(1365678598137754759)
XLA Ops:
  0.0 46.2 %all_gather.3 = s32[1,32,2,128]{3,2,0,1:T(2,128)S(1)} all-gather(s32[1,1,2,128]{3,2,0,1:T(2,128)} %bitcast.172), channel_id=1, replica_groups=mesh['member'=32,'patch'=4,'level'=2] {'member'}, dimensions={1}, use_global_device_ids=true | all-gather | bytes 33792 | tf_op jit(solution)/shard_map/all_gather | solution.py:110
  47.0 10.7 %fusion.7 = f32[8,32,256]{2,0,1:T(8,128)S(1)} fusion(bf16[8,32,12,1024]{3,1,2,0:T(8,128)(2,1)} %bitcast.157, s32[32,256]{1,0:T(8,128)S(1)} %get-tuple-element.6, f32[32,12,256]{2,1,0:T(8,128)S(1)} %fusion.26), kind=kOutput, calls=%fused_computation.12 | convolution fusion | flops 1620508672 | bytes 6979584 | tf_op jit(solution)/shard_map/kpvq,pqo->kpvo/dot_general | solution.py:96
  57.7 4.2 all-reduce.1
  62.6 6.1 %all-to-all-start = ((bf16[8,1,32,2,128]{4,3,0,1,2:T(2,128)(2,1)}), bf16[8,1,32,2,128]{4,3,0,1,2:T(2,128)(2,1)S(1)}, u32[]{:S(2)}, u32[]{:S(2)}) async-start(bf16[8,1,32,2,128]{4,3,0,1,2:T(2,128)(2,1)} %bitcast.38), calls=%async_computation | async-start | bytes 262144 | tf_op jit(solution)/shard_map/all_to_all | solution.py:119
  68.8 9.0 %copy.70 = bf16[8,1,32,1,12,1024]{5,0,4,3,1,2:T(8,128)(2,1)} copy(bf16[8,1,32,1,12,1024]{5,2,4,3,1,0:T(8,128)(2,1)} %param.7) | data formatting | bytes 12582912 | tf_op args[0]
  77.8 1.8 all-to-all-done
  79.6 8.3 %all-to-all-start.1 = ((bf16[8,1,32,1,12,1024]{5,0,4,3,1,2:T(8,128)(2,1)}), bf16[8,1,32,1,12,1024]{5,0,4,3,1,2:T(8,128)(2,1)}, u32[]{:S(2)}, u32[]{:S(2)}) async-start(bf16[8,1,32,1,12,1024]{5,0,4,3,1,2:T(8,128)(2,1)} %copy.70), calls=%async_computation.1 | async-start | bytes 12582912 | tf_op jit(solution)/shard_map/all_to_all | solution.py:118
  89.2 4.6 collective-permute-start
  95.1 4.5 collective-permute-start.4
  99.7 128.2 %collective-permute-done.5 = f32[2,1,1,2,128]{4,3,2,1,0:T(2,128)S(1)} collective-permute-done((f32[2,1,1,2,128]{4,3,2,1,0:T(2,128)S(1)}, f32[2,1,1,2,128]{4,3,2,1,0:T(2,128)S(1)}, u32[]{:S(2)}, u32[]{:S(2)}) %collective-permute-start.5) | collective-permute-done | bytes 2080 | tf_op jit(solution)/shard_map/ppermute | solution.py:27
  227.9 1.7 collective-permute-done.4
  229.6 2.7 collective-permute-start.7
  233.7 4.6 collective-permute-start.3
  238.3 1.5 collective-permute-start.2
  240.0 5.1 %collective-permute-done.3 = bf16[256,1,3,2,128]{4,0,3,2,1:T(8,128)(2,1)S(1)} collective-permute-done((bf16[256,1,3,2,128]{4,0,3,2,1:T(8,128)(2,1)S(1)}, bf16[256,1,3,2,128]{4,0,3,2,1:T(8,128)(2,1)S(1)}, u32[]{:S(2)}, u32[]{:S(2)}) %collective-permute-start.3) | collective-permute-done | bytes 393248 | tf_op jit(solution)/shard_map/ppermute | solution.py:27
  245.1 4.1 collective-permute-done.2
  260.3 4.5 fusion.8
  264.8 4.3 bitcast_convert_fusion
  269.1 4.9 fusion.4
  274.1 8.6 %copy.72 = bf16[256,12288]{0,1:T(8,128)(2,1)} copy(bf16[256,12288]{1,0:T(8,128)(2,1)} %fusion.4) | data formatting | bytes 12582912 | tf_op jit(solution)/shard_map/convert_element_type | solution.py:86
  282.6 11.9 %copy.73 = bf16[256,1,1,1,12,1024]{5,4,3,2,1,0:T(8,128)(2,1)} copy(bf16[256,1,1,1,12,1024]{0,5,4,3,2,1:T(8,128)(2,1)} %bitcast.154) | data formatting | bytes 12582912 | tf_op jit(solution)/shard_map/reshape;stack | solution.py:136
  294.5 194.7 %all_to_all.45 = bf16[256,1,1,1,12,1024]{5,4,3,2,1,0:T(8,128)(2,1)S(1)} all-to-all(bf16[256,1,1,1,12,1024]{5,4,3,2,1,0:T(8,128)(2,1)} %copy.73), channel_id=1, replica_groups=mesh['member'=32,'patch'=4,'level'=2] {'member'}, dimensions={0} | all-to-all | bytes 12582912 | tf_op jit(solution)/shard_map/all_to_all | solution.py:137
  489.3 6.2 %copy.113 = bf16[256,1,1,1,12,1024]{5,0,4,3,2,1:T(8,128)(2,1)} copy(bf16[256,1,1,1,12,1024]{5,4,3,2,1,0:T(8,128)(2,1)S(1)} %all_to_all.45) | data formatting | bytes 12582912 | tf_op jit(solution)/shard_map/all_to_all | solution.py:137
  495.4 9.0 %copy.75 = bf16[8,1,32,1,12,1024]{5,2,4,3,1,0:T(8,128)(2,1)} copy(bf16[8,1,32,1,12,1024]{5,0,2,4,3,1:T(8,128)(2,1)} %bitcast.155) | data formatting | bytes 12582912 | tf_op jit(solution)/shard_map/all_to_all | solution.py:137
  (58 shorter events, 15.9 us)
Async XLA Ops:
  62.6 17.0 %all-to-all-start = ((bf16[8,1,32,2,128]{4,3,0,1,2:T(2,128)(2,1)}), bf16[8,1,32,2,128]{4,3,0,1,2:T(2,128)(2,1)S(1)}, u32[]{:S(2)}, u32[]{:S(2)}) async-start(bf16[8,1,32,2,128]{4,3,0,1,2:T(2,128)(2,1)} %bitcast.38), calls=%async_computation | async-start | bytes 262144 | tf_op jit(solution)/shard_map/all_to_all | solution.py:119
  77.8 10.1 %copy-start.1 = (f32[1,1,2,128]{3,2,1,0:T(2,128)S(1)}, f32[1,1,2,128]{3,2,1,0:T(2,128)}, u32[]{:S(2)}) copy-start(f32[1,1,2,128]{3,2,1,0:T(2,128)} %param.9) | copy-start | bytes 3076
  77.8 10.1 %copy-start.3 = (s32[1,1,2]{2,1,0:T(1,128)S(1)}, s32[1,1,2]{2,1,0:T(1,128)}, u32[]{:S(2)}) copy-start(s32[1,1,2]{2,1,0:T(1,128)} %param.10) | copy-start | bytes 28
  77.8 16.0 %copy-start = (f32[1,1,2,128]{3,2,1,0:T(2,128)S(1)}, f32[1,1,2,128]{3,2,1,0:T(2,128)}, u32[]{:S(2)}) copy-start(f32[1,1,2,128]{3,2,1,0:T(2,128)} %param.8) | copy-start | bytes 3076
  77.8 162.0 %copy-start.2 = (s32[1,1,8]{2,1,0:T(1,128)S(1)}, s32[1,1,8]{2,1,0:T(1,128)}, u32[]{:S(2)}) copy-start(s32[1,1,8]{2,1,0:T(1,128)} %param.13) | copy-start | bytes 100
  79.6 180.7 %all-to-all-start.1 = ((bf16[8,1,32,1,12,1024]{5,0,4,3,1,2:T(8,128)(2,1)}), bf16[8,1,32,1,12,1024]{5,0,4,3,1,2:T(8,128)(2,1)}, u32[]{:S(2)}, u32[]{:S(2)}) async-start(bf16[8,1,32,1,12,1024]{5,0,4,3,1,2:T(8,128)(2,1)} %copy.70), calls=%async_computation.1 | async-start | bytes 12582912 | tf_op jit(solution)/shard_map/all_to_all | solution.py:118
  87.9 145.7 %collective-permute-start.1 = (bf16[256,1,1,2,128]{4,0,3,2,1:T(8,128)(2,1)S(1)}, bf16[256,1,1,2,128]{4,0,3,2,1:T(8,128)(2,1)S(1)}, u32[]{:S(2)}, u32[]{:S(2)}) collective-permute-start(bf16[256,1,1,2,128]{4,0,3,2,1:T(8,128)(2,1)S(1)} %bitcast.161), channel_id=1, source_target_pairs={{8,0},{16,8},{24,16},{32,24},{40,32},{48,40},{56,48},{64,56},{72,6... | collective-permute-start | bytes 393224 | tf_op jit(solution)/shard_map/ppermute | solution.py:27
  89.2 144.4 %collective-permute-start = (bf16[256,1,1,2,128]{4,0,3,2,1:T(8,128)(2,1)S(1)}, bf16[256,1,1,2,128]{4,0,3,2,1:T(8,128)(2,1)S(1)}, u32[]{:S(2)}, u32[]{:S(2)}) collective-permute-start(bf16[256,1,1,2,128]{4,0,3,2,1:T(8,128)(2,1)S(1)} %bitcast.162), channel_id=1, source_target_pairs={{0,8},{8,16},{16,24},{24,32},{32,40},{40,48},{48,56},{56,64},{64,7... | collective-permute-start | bytes 393224 | tf_op jit(solution)/shard_map/ppermute | solution.py:25
  93.8 134.1 %collective-permute-start.5 = (f32[2,1,1,2,128]{4,3,2,1,0:T(2,128)S(1)}, f32[2,1,1,2,128]{4,3,2,1,0:T(2,128)S(1)}, u32[]{:S(2)}, u32[]{:S(2)}) collective-permute-start(f32[2,1,1,2,128]{4,3,2,1,0:T(2,128)S(1)} %pad_maximum_fusion.4), channel_id=1, source_target_pairs={{8,0},{16,8},{24,16},{32,24},{40,32},{48,40},{56,48},{64,56},{72,6... | collective-permute-start | bytes 6152 | tf_op jit(solution)/shard_map/ppermute | solution.py:27
  95.1 134.5 %collective-permute-start.4 = (f32[2,1,1,2,128]{4,3,2,1,0:T(2,128)S(1)}, f32[2,1,1,2,128]{4,3,2,1,0:T(2,128)S(1)}, u32[]{:S(2)}, u32[]{:S(2)}) collective-permute-start(f32[2,1,1,2,128]{4,3,2,1,0:T(2,128)S(1)} %pad_maximum_fusion.4), channel_id=1, source_target_pairs={{0,8},{8,16},{16,24},{24,32},{32,40},{40,48},{48,56},{56,64},{64,7... | collective-permute-start | bytes 6152 | tf_op jit(solution)/shard_map/ppermute | solution.py:25
  229.6 10.2 %collective-permute-start.7 = (f32[2,1,3,2,128]{4,3,2,1,0:T(2,128)S(1)}, f32[2,1,3,2,128]{4,3,2,1,0:T(2,128)S(1)}, u32[]{:S(2)}, u32[]{:S(2)}) collective-permute-start(f32[2,1,3,2,128]{4,3,2,1,0:T(2,128)S(1)} %pad_maximum_fusion.3), channel_id=1, source_target_pairs={{2,0},{4,2},{6,4},{3,1},{5,3},{7,5},{10,8},{12,10},{14,12},{11,9},... | collective-permute-start | bytes 18440 | tf_op jit(solution)/shard_map/ppermute | solution.py:27
  232.3 7.5 %collective-permute-start.6 = (f32[2,1,3,2,128]{4,3,2,1,0:T(2,128)S(1)}, f32[2,1,3,2,128]{4,3,2,1,0:T(2,128)S(1)}, u32[]{:S(2)}, u32[]{:S(2)}) collective-permute-start(f32[2,1,3,2,128]{4,3,2,1,0:T(2,128)S(1)} %pad_maximum_fusion.3), channel_id=1, source_target_pairs={{0,2},{2,4},{4,6},{1,3},{3,5},{5,7},{8,10},{10,12},{12,14},{9,11},... | collective-permute-start | bytes 18440 | tf_op jit(solution)/shard_map/ppermute | solution.py:25
  233.7 11.4 %collective-permute-start.3 = (bf16[256,1,3,2,128]{4,0,3,2,1:T(8,128)(2,1)S(1)}, bf16[256,1,3,2,128]{4,0,3,2,1:T(8,128)(2,1)S(1)}, u32[]{:S(2)}, u32[]{:S(2)}) collective-permute-start(bf16[256,1,3,2,128]{4,0,3,2,1:T(8,128)(2,1)S(1)} %pad_maximum_fusion.1), channel_id=1, source_target_pairs={{2,0},{4,2},{6,4},{3,1},{5,3},{7,5},{10,8},{12,10},{14,12},{11,9},... | collective-permute-start | bytes 1179656 | tf_op jit(solution)/shard_map/ppermute | solution.py:27
  238.3 11.0 %collective-permute-start.2 = (bf16[256,1,3,2,128]{4,0,3,2,1:T(8,128)(2,1)S(1)}, bf16[256,1,3,2,128]{4,0,3,2,1:T(8,128)(2,1)S(1)}, u32[]{:S(2)}, u32[]{:S(2)}) collective-permute-start(bf16[256,1,3,2,128]{4,0,3,2,1:T(8,128)(2,1)S(1)} %pad_maximum_fusion.1), channel_id=1, source_target_pairs={{0,2},{2,4},{4,6},{1,3},{3,5},{5,7},{8,10},{10,12},{12,14},{9,11},... | collective-permute-start | bytes 1179656 | tf_op jit(solution)/shard_map/ppermute | solution.py:25
where the time goes:
time: 506 us; the launch traced here: 504 us
  blocking collectives  245 us (48%)
  waiting for transfers between devices  141 us (28%)
  local copies, waits for them, and re-layouts  45.5 us (9%)
  starting transfers between devices  36.1 us (7%)
  matrix products  25.3 us (5%)
  other arithmetic  10.2 us (2%)
    all_to_all x1, blocking collectives, body(): lax.all_to_all(analysed, 'member', split_axis=0, concat_axis=2, tiled=True)  195 us
    ppermute x4, waiting for transfers between devices, extended(): lax.ppermute(head, axis, [((i + 1) % count, i) for i in range(ends)])  133 us
    all_gather x1, blocking collectives, body(): where_all = lax.all_gather(position, 'member', axis=1, tiled=True)  46.2 us
    all_to_all x2, local copies, waits for them, and re-layouts, body(): lax.all_to_all(analysed, 'member', split_axis=0, concat_axis=2, tiled=True)  15.2 us
    another operation x1, local copies, waits for them, and re-layouts, body(): jnp.stack(results, axis=1)  11.9 us
    ppermute x4, starting transfers between devices, extended(): lax.ppermute(tail, axis, [(i, (i + 1) % count) for i in range(ends)])  11.9 us
    dot_general x1, matrix products, observe(): jnp.einsum('kpvq,pqo->kpvo', shaped_fields, column_hot, preferred_element...  10.7 us
  transfers between devices with their start and end apart: 10, of which 6 were waited for; matrix products, arithmetic and copies ran while one was open for 4% of the time, Pallas kernels for 0%

commit v1 on v0

v1 whole, which is shorter than its diff:
```python
import jax
import jax.numpy as jnp
from jax import lax
from jax.experimental import pallas as pl
from jax.experimental.pallas import tpu as pltpu
from jax.sharding import PartitionSpec as P

VARIABLES = 12
COLUMNS = 1024
SLOTS = 128
OWN_BLOCKS = 2
LISTED = 8
SWEEPS = 6
FIRST = 2

exact_precision = lax.Precision.HIGHEST
barrier = lax.optimization_barrier


def exchange(cells):
    return lax.all_to_all(cells, "member", split_axis=0, concat_axis=0, tiled=True)


def row_halo(cells):
    count = lax.axis_size("patch")
    above = lax.ppermute(cells, "patch", [(i, i + 1) for i in range(count - 1)])
    below = lax.ppermute(cells, "patch", [(i + 1, i) for i in range(count - 1)])
    return above, below


def taper_of(listed):
    stepped = listed // OWN_BLOCKS
    moved = jnp.abs(stepped // 3 - 1) + jnp.abs(stepped % 3 - 1)
    return jnp.where(moved == 0, 1.0, jnp.where(moved == 1, 0.6, 0.35)).astype(jnp.float32)


def weights_for(candidates, pairs, listed):
    members = candidates.shape[0]
    candidate_count = candidates.shape[1]
    choose_iota = lax.broadcasted_iota(jnp.int32, (LISTED, candidate_count), 1)
    selector = listed[:, None] == choose_iota
    chosen = jnp.concatenate(
        [
            lax.dynamic_slice_in_dim(candidates, listed[j], 1, axis=1).reshape(members, SLOTS)
            for j in range(LISTED)
        ],
        axis=1,
    )
    picked = jnp.einsum(
        "ajs,lj->als", pairs, selector.astype(jnp.float32), precision=exact_precision
    )
    tapering = taper_of(listed)
    widened = barrier(chosen).astype(jnp.float32)
    centre = jnp.mean(widened, axis=0)
    obs_pert = (widened - centre).astype(jnp.bfloat16)
    weight = (picked[1] * tapering[:, None]).reshape(LISTED * SLOTS)
    innovation = picked[0].reshape(LISTED * SLOTS) - centre
    pert_wide = barrier(obs_pert).astype(jnp.float32)
    scaled = (pert_wide * jnp.sqrt(weight)).astype(jnp.bfloat16)
    identity = jnp.eye(members, dtype=jnp.float32)
    system = lax.dot_general(
        scaled, scaled, (((1,), (1,)), ((), ())), preferred_element_type=jnp.float32
    )
    system = system + (members - 1) / 1.1 * identity
    scaling = jnp.sqrt(jnp.sum(system * system))
    iterate = system / scaling
    inverse_root = identity
    for iteration in range(SWEEPS):
        middle = 1.5 * identity - 0.5 * jnp.dot(inverse_root, iterate, precision=exact_precision)
        iterate = jnp.dot(iterate, middle, precision=exact_precision)
        inverse_root = jnp.dot(middle, inverse_root, precision=exact_precision)
    forcing = jnp.dot(pert_wide, weight * innovation, precision=exact_precision)
    inner = jnp.dot(inverse_root, forcing, precision=exact_precision)
    mean_weight = jnp.dot(inverse_root, inner, precision=exact_precision) / scaling
    weights = jnp.sqrt((members - 1) / scaling) * inverse_root + mean_weight[:, None]
    return weights.astype(jnp.bfloat16).T


def apply_kernel(weights_ref, fields_ref, out_ref):
    sources, _, own, columns = fields_ref.shape
    members = sources * own
    wide = fields_ref[...].reshape(sources, own, columns).astype(jnp.float32).reshape(members, columns)
    mean = jnp.sum(wide, axis=0, keepdims=True) * (1.0 / members)
    pert = (wide - mean).astype(jnp.bfloat16)
    updated = jnp.dot(weights_ref[...], pert, preferred_element_type=jnp.float32) + mean
    out_ref[...] = updated.reshape(sources, 1, own, columns).astype(out_ref.dtype)


def apply_weights(weights, fields):
    sources, levels, own, columns = fields.shape
    members = sources * own
    block = pl.BlockSpec((sources, 1, own, columns), lambda v: (0, v, 0, 0))
    return pl.pallas_call(
        apply_kernel,
        grid=(levels,),
        in_specs=[pl.BlockSpec((members, members), lambda v: (0, 0)), block],
        out_specs=block,
        out_shape=jax.ShapeDtypeStruct(fields.shape, fields.dtype),
        compiler_params=pltpu.CompilerParams(vmem_limit_bytes=24 * 1024 * 1024),
        cost_estimate=pl.CostEstimate(
            flops=2 * members * members * levels * columns,
            bytes_accessed=4 * members * levels * columns,
            transcendentals=0,
        ),
    )(weights, fields)


def observe(shaped_fields, where_flat, kernel):
    patch_count = where_flat.shape[0]
    slot_count = where_flat.shape[1]
    column_of = where_flat % COLUMNS
    variable_of = where_flat // COLUMNS
    column_iota = lax.broadcasted_iota(jnp.int32, (patch_count, COLUMNS, slot_count), 1)
    column_hot = (column_of[:, None, :] == column_iota).astype(jnp.bfloat16)
    spread = jnp.einsum(
        "kpvq,pqo->kpvo", shaped_fields, column_hot, preferred_element_type=jnp.float32
    )
    variable_iota = lax.broadcasted_iota(jnp.int32, (patch_count, VARIABLES, slot_count), 1)
    variable_weight = jnp.where(
        variable_of[:, None, :] == variable_iota, kernel[None, :, None], 0.0
    )
    return jnp.sum(spread * variable_weight[None], axis=2)


def body(ensemble, observations, precision, valid_count, position, level_kernel, listed_blocks):
    kernel = level_kernel[0]
    own = ensemble.shape[0]
    row_patches = ensemble.shape[2]
    members = own * row_patches
    fields = ensemble.reshape(own, row_patches, VARIABLES, COLUMNS)

    slot_index = lax.broadcasted_iota(jnp.int32, precision.shape, 3)
    precision_used = jnp.where(slot_index < valid_count[..., None], precision, 0.0)
    table = jnp.concatenate(
        [
            position.reshape(OWN_BLOCKS, SLOTS).astype(jnp.float32),
            observations.reshape(OWN_BLOCKS, SLOTS),
            precision_used.reshape(OWN_BLOCKS, SLOTS),
        ]
    )
    tables = exchange(jnp.broadcast_to(table[None], (row_patches,) + table.shape))

    def outgoing(low, high):
        return fields[:, :, low:high].transpose(1, 2, 0, 3)

    first = outgoing(0, FIRST)
    first, tables = barrier((first, tables))
    first = exchange(first)

    where = tables[:, :OWN_BLOCKS].reshape(row_patches, OWN_BLOCKS * SLOTS).astype(jnp.int32)
    level_term = observe(fields, where, kernel)
    equivalent = lax.psum(level_term, "level").astype(jnp.bfloat16)
    padded = jnp.pad(equivalent, ((0, 0), (1, 1), (0, 0)))
    spread = jnp.concatenate(
        [padded[:, shift : shift + row_patches] for shift in range(3)], axis=2
    ).transpose(1, 0, 2)
    spread, first = barrier((spread, first))
    near = exchange(spread).reshape(members, 3 * OWN_BLOCKS * SLOTS)

    rest = outgoing(FIRST, VARIABLES)
    rest, near = barrier((rest, near))
    rest = exchange(rest)

    here = lax.axis_index("member")
    pair_rows = jnp.pad(tables[:, OWN_BLOCKS:], ((1, 1), (0, 0), (0, 0)))
    pair_own = lax.dynamic_slice_in_dim(pair_rows, here, 3, axis=0)
    pair_above, pair_below = row_halo(pair_own)
    near_above, near_below = row_halo(near)
    candidates = jnp.concatenate([near_above, near, near_below], axis=1)
    candidates = candidates.reshape(members, 9 * OWN_BLOCKS, SLOTS)
    pairs = jnp.concatenate([pair_above, pair_own, pair_below], axis=0)
    pairs = pairs.reshape(9, 2, OWN_BLOCKS, SLOTS).transpose(1, 0, 2, 3)
    pairs = pairs.reshape(2, 9 * OWN_BLOCKS, SLOTS)
    weights = weights_for(candidates, pairs, listed_blocks[0, 0])

    first_out = apply_weights(weights, first)
    first_out, rest = barrier((first_out, rest))
    first_back = exchange(first_out)
    rest_out = apply_weights(weights, rest)
    rest_out, first_back = barrier((rest_out, first_back))
    rest_back = exchange(rest_out)
    result = jnp.concatenate([first_back, rest_back], axis=1)
    result = result.transpose(2, 0, 1, 3)
    return result.reshape(ensemble.shape)


def solution(mesh):
    placed = (
        P("member", "patch", None, "level", None, None),
        P("patch", "member", None, None),
        P("patch", "member", None, None),
        P("patch", "member", None),
        P("patch", "member", None, None),
        P("level", None),
        P("patch", "member", None),
    )
    return jax.shard_map(
        body,
        mesh=mesh,
        in_specs=placed,
        out_specs=P("member", "patch", None, "level", None, None),
        check_vma=False,
    )
```

time: 506 us -> 370 us (0.73)
  blocking collectives: 245 us -> 127 us
  waiting for transfers between devices: 141 us -> 116 us
  local copies, waits for them, and re-layouts: 45.5 us -> 27.6 us
  between operations: 1.24 us -> 16.4 us
  starting transfers between devices: 36.1 us -> 48.2 us
  Pallas kernels: 0 us -> 9.94 us
  matrix products: 25.3 us -> 19.2 us
  other arithmetic: 10.2 us -> 4.13 us
    ppermute x8 -> x4, waiting for transfers between devices: 139 us -> 0.01 us  [the longest x2 0.01 us: row_halo(): above = lax.ppermute(cells, 'patch', [(i, i + 1) for i in range(count - 1)])]
    all_to_all x2 -> x5, waiting for transfers between devices: 1.85 us -> 116 us  [exchange(): lax.all_to_all(cells, 'member', split_axis=0, concat_axis=0, tiled=True)]
    all_to_all x1, blocking collectives: 195 us -> 123 us  [exchange(): lax.all_to_all(cells, 'member', split_axis=0, concat_axis=0, tiled=True)]
    all_gather x1 -> x0, blocking collectives: 46.2 us -> none  [body(): where_all = lax.all_gather(position, 'member', axis=1, tiled=True)]
    all_to_all x2 -> x5, starting transfers between devices: 14.4 us -> 38.1 us  [exchange(): lax.all_to_all(cells, 'member', split_axis=0, concat_axis=0, tiled=True)]
    all_to_all x3 -> x0, local copies, waits for them, and re-layouts: 15.2 us -> none  [the longest x2 15.2 us: body(): lax.all_to_all(analysed, 'member', split_axis=0, concat_axis=2, tiled=True)]
    another operation x1 -> x0, local copies, waits for them, and re-layouts: 11.9 us -> none  [body(): jnp.stack(results, axis=1)]
    ppermute x8 -> x4, starting transfers between devices: 21.7 us -> 10.1 us  [the longest x2 7.3 us: row_halo(): below = lax.ppermute(cells, 'patch', [(i + 1, i) for i in range(count - 1)])]
  transfers between devices with their start and end apart: 10 -> 9, of which waited for: 6 -> 5; matrix products, arithmetic and copies ran while one was open for 4% -> 10% of each run, Pallas kernels for 0% -> 3%
where the time goes in v1:
time: 370 us; the launch traced here: 368 us
  blocking collectives  127 us (34%)
  waiting for transfers between devices  116 us (31%)
  starting transfers between devices  48.2 us (13%)
  local copies, waits for them, and re-layouts  27.6 us (7%)
  matrix products  19.2 us (5%)
  between operations  16.4 us (4%)
  Pallas kernels  9.94 us (3%)
  other arithmetic  4.13 us (1%)
    all_to_all x1, blocking collectives, exchange(): lax.all_to_all(cells, 'member', split_axis=0, concat_axis=0, tiled=True)  123 us
    all_to_all x5, waiting for transfers between devices, exchange(): lax.all_to_all(cells, 'member', split_axis=0, concat_axis=0, tiled=True)  116 us
    all_to_all x5, starting transfers between devices, exchange(): lax.all_to_all(cells, 'member', split_axis=0, concat_axis=0, tiled=True)  38.1 us
    unnamed x16, local copies, waits for them, and re-layouts  11.5 us
    dot_general x1, matrix products, observe(): jnp.einsum('kpvq,pqo->kpvo', shaped_fields, column_hot, preferred_element...  10.7 us
    pallas_call x2, Pallas kernels, apply_weights(): pl.pallas_call(apply_kernel, grid=(levels,), in_specs=[pl.BlockSpec((memb...  9.94 us
  transfers between devices with their start and end apart: 9, of which 5 were waited for; matrix products, arithmetic and copies ran while one was open for 10% of the time, Pallas kernels for 3%

profile of v1, /device:TPU:6, one launch (start us, length us, event | category | flops | bytes accessed | tf_op | source)
XLA Modules:
  0.0 368.4 jit_solution(9132020947217288426)
XLA Ops:
  2.8 11.5 %all-to-all-start = ((f32[32,6,128]{2,1,0:T(8,128)}), f32[32,6,128]{2,1,0:T(8,128)S(1)}, u32[]{:S(2)}, u32[]{:S(2)}) async-start(f32[32,6,128]{2,1,0:T(8,128)} %broadcast_in_dim.45), calls=%async_computation | async-start | bytes 262144 | tf_op jit(solution)/shard_map/all_to_all | solution.py:21
  14.3 6.3 %copy.56 = bf16[8,1,32,1,12,1024]{5,0,4,2,3,1:T(8,128)(2,1)S(1)} copy(bf16[8,1,32,1,12,1024]{5,2,4,3,1,0:T(8,128)(2,1)} %param.7) | data formatting | bytes 12582912 | tf_op args[0]
  20.6 2.7 copy-done.1
  23.3 1.0 slice_bitcast_fusion.1
  24.6 9.6 %all-to-all-start.1 = ((bf16[32,2,8,1024]{3,2,1,0:T(8,128)(2,1)}), bf16[32,2,8,1024]{3,2,1,0:T(8,128)(2,1)S(1)}, u32[]{:S(2)}, u32[]{:S(2)}) async-start(bf16[32,2,8,1024]{3,2,1,0:T(8,128)(2,1)} %slice_bitcast_fusion.1), calls=%async_computation.1 | async-start | bytes 2097152 | tf_op jit(solution)/shard_map/all_to_all | solution.py:21
  34.3 10.7 %fusion.5 = f32[8,32,256]{2,0,1:T(8,128)S(1)} fusion(bf16[8,32,12,1024]{3,1,2,0:T(8,128)(2,1)} %bitcast.164, s32[32,256]{1,0:T(8,128)S(1)} %get-tuple-element.36, f32[32,12,256]{2,1,0:T(8,128)S(1)} %fusion.18), kind=kOutput, calls=%fused_computation.9 | convolution fusion | flops 1620508672 | bytes 6979584 | tf_op jit(solution)/shard_map/kpvq,pqo->kpvo/dot_general | solution.py:115
  45.0 4.2 %all-reduce.3 = bf16[8,32,256]{2,0,1:T(8,128)(2,1)S(1)} all-reduce(f32[8,32,256]{2,0,1:T(8,128)S(1)} %fusion.5), channel_id=1, replica_groups=mesh['member'=32,'patch'=4,'level'=2] {'level'}, use_global_device_ids=true, to_apply=%region_1.2 | all-reduce | flops 65536 | bytes 393216 | tf_op jit(solution)/shard_map/psum | solution.py:152
  50.0 12.4 %all-to-all-done.1.fields_ref = bf16[32,2,8,1024]{3,2,1,0:T(8,128)(2,1)S(1)} async-done(((bf16[32,2,8,1024]{3,2,1,0:T(8,128)(2,1)}), bf16[32,2,8,1024]{3,2,1,0:T(8,128)(2,1)S(1)}, u32[]{:S(2)}, u32[]{:S(2)}) %all-to-all-start.1) | async-done | bytes 1048608 | tf_op jit(solution)/shard_map/all_to_all | solution.py:21
  62.5 4.9 %all-to-all-start.2 = ((bf16[32,8,768]{2,1,0:T(8,128)(2,1)}), bf16[32,8,768]{2,1,0:T(8,128)(2,1)S(1)}, u32[]{:S(2)}, u32[]{:S(2)}) async-start(bf16[32,8,768]{2,1,0:T(8,128)(2,1)} %maximum_bitcast_fusion.1), calls=%async_computation.2 | async-start | bytes 786432 | tf_op jit(solution)/shard_map/all_to_all | solution.py:21
  67.4 5.7 %slice_bitcast_fusion = bf16[32,10,8,1024]{3,2,1,0:T(8,128)(2,1)} fusion(bf16[8,32,12,1024]{3,0,2,1:T(8,128)(2,1)} %bitcast.163), kind=kLoop, calls=%fused_computation.7 | loop fusion | bytes 10485760 | tf_op jit(solution)/shard_map/transpose | solution.py:144
  73.1 8.2 %all-to-all-done.2 = bf16[32,8,768]{2,1,0:T(8,128)(2,1)S(1)} async-done(((bf16[32,8,768]{2,1,0:T(8,128)(2,1)}), bf16[32,8,768]{2,1,0:T(8,128)(2,1)S(1)}, u32[]{:S(2)}, u32[]{:S(2)}) %all-to-all-start.2) | async-done | bytes 393248 | tf_op jit(solution)/shard_map/all_to_all | solution.py:21
  81.3 5.5 %all-to-all-start.3 = ((bf16[32,10,8,1024]{3,2,1,0:T(8,128)(2,1)}), bf16[32,10,8,1024]{3,2,1,0:T(8,128)(2,1)}, u32[]{:S(2)}, u32[]{:S(2)}) async-start(bf16[32,10,8,1024]{3,2,1,0:T(8,128)(2,1)} %slice_bitcast_fusion), calls=%async_computation.3 | async-start | bytes 10485760 | tf_op jit(solution)/shard_map/all_to_all | solution.py:21
  86.9 2.7 collective-permute-start.3
  89.6 1.3 collective-permute-start.2
  90.9 4.6 %collective-permute-start.1 = (bf16[256,768]{1,0:T(8,128)(2,1)S(1)}, bf16[256,768]{1,0:T(8,128)(2,1)S(1)}, u32[]{:S(2)}, u32[]{:S(2)}) collective-permute-start(bf16[256,768]{1,0:T(8,128)(2,1)S(1)} %bitcast.166), channel_id=1, source_target_pairs={{2,0},{4,2},{6,4},{3,1},{5,3},{7,5},{10,8},{12,10},{14,12},{11,9},... | collective-permute-start | bytes 1179656 | tf_op jit(solution)/shard_map/ppermute | solution.py:27
  95.5 1.5 collective-permute-start
  124.7 1.8 shard_map.76
  126.5 76.7 %all-to-all-done.3.fields_ref = bf16[32,10,8,1024]{3,2,1,0:T(8,128)(2,1)} async-done(((bf16[32,10,8,1024]{3,2,1,0:T(8,128)(2,1)}), bf16[32,10,8,1024]{3,2,1,0:T(8,128)(2,1)}, u32[]{:S(2)}, u32[]{:S(2)}) %all-to-all-start.3) | async-done | bytes 5242912 | tf_op jit(solution)/shard_map/all_to_all | solution.py:21
  203.3 6.7 %all-to-all-start.4 = ((bf16[32,2,8,1024]{3,2,1,0:T(8,128)(2,1)}), bf16[32,2,8,1024]{3,2,1,0:T(8,128)(2,1)S(1)}, u32[]{:S(2)}, u32[]{:S(2)}) async-start(bf16[32,2,8,1024]{3,2,1,0:T(8,128)(2,1)} %shard_map.76), calls=%async_computation.4 | async-start | bytes 2097152 | tf_op jit(solution)/shard_map/all_to_all | solution.py:21
  210.0 8.1 %shard_map.77 = bf16[32,10,8,1024]{3,2,1,0:T(8,128)(2,1)S(1)} custom-call(bf16[256,256]{1,0:T(8,128)(2,1)S(1)} %fusion.20.weights_ref, bf16[32,10,8,1024]{3,2,1,0:T(8,128)(2,1)} %all-to-all-done.3.fields_ref), custom_call_target="tpu_custom_call" | custom-call | flops 1342177280 | bytes 10485760 | tf_op jit(solution)/shard_map/pallas_call | solution.py:93
  218.2 2.3 copy-done
  220.5 18.0 %all-to-all-done.4 = bf16[32,2,8,1024]{3,2,1,0:T(8,128)(2,1)S(1)} async-done(((bf16[32,2,8,1024]{3,2,1,0:T(8,128)(2,1)}), bf16[32,2,8,1024]{3,2,1,0:T(8,128)(2,1)S(1)}, u32[]{:S(2)}, u32[]{:S(2)}) %all-to-all-start.4) | async-done | bytes 1048608 | tf_op jit(solution)/shard_map/all_to_all | solution.py:21
  238.5 123.1 %all_to_all.30 = bf16[32,10,8,1024]{3,2,1,0:T(8,128)(2,1)S(1)} all-to-all(bf16[32,10,8,1024]{3,2,1,0:T(8,128)(2,1)} %copy-done), channel_id=1, replica_groups=mesh['member'=32,'patch'=4,'level'=2] {'member'}, dimensions={0} | all-to-all | bytes 10485760 | tf_op jit(solution)/shard_map/all_to_all | solution.py:21
  362.1 6.2 %copy.26 = bf16[8,1,32,1,12,1024]{5,2,4,3,1,0:T(8,128)(2,1)} copy(bf16[8,1,32,1,12,1024]{5,0,4,2,3,1:T(8,128)(2,1)S(1)} %maximum_bitcast_fusion) | data formatting | bytes 12582912 | tf_op jit(solution)/shard_map/reshape | solution.py:184
  (74 shorter events, 16.2 us)
Async XLA Ops:
  2.8 21.8 %all-to-all-start = ((f32[32,6,128]{2,1,0:T(8,128)}), f32[32,6,128]{2,1,0:T(8,128)S(1)}, u32[]{:S(2)}, u32[]{:S(2)}) async-start(f32[32,6,128]{2,1,0:T(8,128)} %broadcast_in_dim.45), calls=%async_computation | async-start | bytes 262144 | tf_op jit(solution)/shard_map/all_to_all | solution.py:21
  14.3 19.9 %copy-start.3 = (f32[1,12]{1,0:T(1,128)S(1)}, f32[1,12]{1,0:T(1,128)}, u32[]{:S(2)}) copy-start(f32[1,12]{1,0:T(1,128)} %param.12) | copy-start | bytes 148
  20.6 2.7 copy-start.1
  24.6 37.9 %all-to-all-start.1 = ((bf16[32,2,8,1024]{3,2,1,0:T(8,128)(2,1)}), bf16[32,2,8,1024]{3,2,1,0:T(8,128)(2,1)S(1)}, u32[]{:S(2)}, u32[]{:S(2)}) async-start(bf16[32,2,8,1024]{3,2,1,0:T(8,128)(2,1)} %slice_bitcast_fusion.1), calls=%async_computation.1 | async-start | bytes 2097152 | tf_op jit(solution)/shard_map/all_to_all | solution.py:21
  62.5 18.8 %all-to-all-start.2 = ((bf16[32,8,768]{2,1,0:T(8,128)(2,1)}), bf16[32,8,768]{2,1,0:T(8,128)(2,1)S(1)}, u32[]{:S(2)}, u32[]{:S(2)}) async-start(bf16[32,8,768]{2,1,0:T(8,128)(2,1)} %maximum_bitcast_fusion.1), calls=%async_computation.2 | async-start | bytes 786432 | tf_op jit(solution)/shard_map/all_to_all | solution.py:21
  81.3 5.5 %copy-start.2 = (s32[1,1,8]{2,1,0:T(1,128)S(1)}, s32[1,1,8]{2,1,0:T(1,128)}, u32[]{:S(2)}) copy-start(s32[1,1,8]{2,1,0:T(1,128)} %param.13) | copy-start | bytes 100
  81.3 122.0 %all-to-all-start.3 = ((bf16[32,10,8,1024]{3,2,1,0:T(8,128)(2,1)}), bf16[32,10,8,1024]{3,2,1,0:T(8,128)(2,1)}, u32[]{:S(2)}, u32[]{:S(2)}) async-start(bf16[32,10,8,1024]{3,2,1,0:T(8,128)(2,1)} %slice_bitcast_fusion), calls=%async_computation.3 | async-start | bytes 10485760 | tf_op jit(solution)/shard_map/all_to_all | solution.py:21
  86.9 25.8 %collective-permute-start.3 = (f32[3,4,128]{2,1,0:T(4,128)S(1)}, f32[3,4,128]{2,1,0:T(4,128)S(1)}, u32[]{:S(2)}, u32[]{:S(2)}) collective-permute-start(f32[3,4,128]{2,1,0:T(4,128)S(1)} %pad_dynamic-slice_fusion), channel_id=1, source_target_pairs={{2,0},{4,2},{6,4},{3,1},{5,3},{7,5},{10,8},{12,10},{14,12},{11,9},... | collective-permute-start | bytes 18440 | tf_op jit(solution)/shard_map/ppermute | solution.py:27
  89.6 23.1 %collective-permute-start.2 = (f32[3,4,128]{2,1,0:T(4,128)S(1)}, f32[3,4,128]{2,1,0:T(4,128)S(1)}, u32[]{:S(2)}, u32[]{:S(2)}) collective-permute-start(f32[3,4,128]{2,1,0:T(4,128)S(1)} %pad_dynamic-slice_fusion), channel_id=1, source_target_pairs={{0,2},{2,4},{4,6},{1,3},{3,5},{5,7},{8,10},{10,12},{12,14},{9,11},... | collective-permute-start | bytes 18440 | tf_op jit(solution)/shard_map/ppermute | solution.py:26
  90.9 22.0 %collective-permute-start.1 = (bf16[256,768]{1,0:T(8,128)(2,1)S(1)}, bf16[256,768]{1,0:T(8,128)(2,1)S(1)}, u32[]{:S(2)}, u32[]{:S(2)}) collective-permute-start(bf16[256,768]{1,0:T(8,128)(2,1)S(1)} %bitcast.166), channel_id=1, source_target_pairs={{2,0},{4,2},{6,4},{3,1},{5,3},{7,5},{10,8},{12,10},{14,12},{11,9},... | collective-permute-start | bytes 1179656 | tf_op jit(solution)/shard_map/ppermute | solution.py:27
  95.5 17.5 %collective-permute-start = (bf16[256,768]{1,0:T(8,128)(2,1)S(1)}, bf16[256,768]{1,0:T(8,128)(2,1)S(1)}, u32[]{:S(2)}, u32[]{:S(2)}) collective-permute-start(bf16[256,768]{1,0:T(8,128)(2,1)S(1)} %bitcast.167), channel_id=1, source_target_pairs={{0,2},{2,4},{4,6},{1,3},{3,5},{5,7},{8,10},{10,12},{12,14},{9,11},... | collective-permute-start | bytes 1179656 | tf_op jit(solution)/shard_map/ppermute | solution.py:26
  203.3 35.2 %all-to-all-start.4 = ((bf16[32,2,8,1024]{3,2,1,0:T(8,128)(2,1)}), bf16[32,2,8,1024]{3,2,1,0:T(8,128)(2,1)S(1)}, u32[]{:S(2)}, u32[]{:S(2)}) async-start(bf16[32,2,8,1024]{3,2,1,0:T(8,128)(2,1)} %shard_map.76), calls=%async_computation.4 | async-start | bytes 2097152 | tf_op jit(solution)/shard_map/all_to_all | solution.py:21
  218.1 2.4 copy-start

commit v2 on v1

v2 whole, which is shorter than its diff:
```python
import jax
import jax.numpy as jnp
from jax import lax
from jax.experimental import pallas as pl
from jax.experimental.pallas import tpu as pltpu
from jax.sharding import PartitionSpec as P

VARIABLES = 12
COLUMNS = 1024
SLOTS = 128
OWN_BLOCKS = 2
LISTED = 8
SWEEPS = 6
FIRST = 4
STEP = 4
DEPTHS = 8
TURNS = 4

exact_precision = lax.Precision.HIGHEST
barrier = lax.optimization_barrier


def exchange(cells):
    return lax.all_to_all(cells, "member", split_axis=0, concat_axis=0, tiled=True)


def row_halo(cells):
    count = lax.axis_size("patch")
    above = lax.ppermute(cells, "patch", [(i, i + 1) for i in range(count - 1)])
    below = lax.ppermute(cells, "patch", [(i + 1, i) for i in range(count - 1)])
    return above, below


def shifted(cells, turn, depth):
    pairs = []
    for y in range(TURNS):
        for z in range(DEPTHS):
            pairs.append((y * DEPTHS + z, (y + turn) % TURNS * DEPTHS + (z + depth) % DEPTHS))
    return lax.ppermute(cells, "member", pairs)


def swapped(cells):
    return lax.ppermute(cells, "level", [(0, 1), (1, 0)])


def cost(values, flops=0):
    return pl.CostEstimate(flops=flops, bytes_accessed=4 * values, transcendentals=0)


WEIGHTS_COST = pl.CostEstimate(flops=0, bytes_accessed=1024, transcendentals=0)
PARAMS = pltpu.CompilerParams(vmem_limit_bytes=56 * 1024 * 1024)
SMALL = pltpu.CompilerParams(vmem_limit_bytes=32 * 1024 * 1024)


def weights_kernel(listed_ref, place_ref, *refs):
    own_refs, other_refs, pair_refs = refs[:3], refs[3:6], refs[6:9]
    weights_ref, sided_ref, scaled_ref = refs[9:]
    members = own_refs[0].shape[0]
    total = jnp.zeros((members, SLOTS), jnp.float32)
    for j in range(LISTED):
        block = listed_ref[j]
        row = lax.div(block, 3 * OWN_BLOCKS)
        inside = lax.rem(block, 3 * OWN_BLOCKS)
        column = lax.div(inside, OWN_BLOCKS)
        which = lax.rem(inside, OWN_BLOCKS)
        away = jnp.abs(row - 1) + jnp.abs(column - 1)
        taper = jnp.where(away == 0, 1.0, jnp.where(away == 1, 0.6, 0.35)).astype(jnp.float32)
        lanes = pl.ds(pl.multiple_of(column * SLOTS, SLOTS), SLOTS)
        near_refs = zip(own_refs, other_refs)
        wide = [
            jnp.where(
                which == place_ref[2],
                own_ref[:, lanes].astype(jnp.float32),
                other_ref[:, lanes].astype(jnp.float32),
            )
            for own_ref, other_ref in near_refs
        ]
        wide = jnp.where(row == 0, wide[0], jnp.where(row == 1, wide[1], wide[2]))
        pair = [ref[column] for ref in pair_refs]
        pair = jnp.where(row == 0, pair[0], jnp.where(row == 1, pair[1], pair[2]))
        observed = jnp.where(which == 0, pair[0:1], pair[1:2])
        weight = jnp.where(which == 0, pair[2:3], pair[3:4]) * taper
        centre = jnp.sum(wide, axis=0, keepdims=True) * (1.0 / members)
        pert = (wide - centre).astype(jnp.bfloat16).astype(jnp.float32)
        scaled_ref[:, j * SLOTS : (j + 1) * SLOTS] = (pert * jnp.sqrt(weight)).astype(jnp.bfloat16)
        total = total + pert * (weight * (observed - centre))
    forcing = jnp.sum(total, axis=1, keepdims=True)
    scaled = scaled_ref[...]
    system = lax.dot_general(
        scaled, scaled, (((1,), (1,)), ((), ())), preferred_element_type=jnp.float32
    )
    rows = lax.broadcasted_iota(jnp.int32, (members, members), 0)
    columns = lax.broadcasted_iota(jnp.int32, (members, members), 1)
    identity = jnp.where(rows == columns, 1.0, 0.0).astype(jnp.float32)
    system = system + (members - 1) / 1.1 * identity
    scaling = jnp.sqrt(
        jnp.sum(jnp.sum(system * system, axis=1, keepdims=True), axis=0, keepdims=True)
    )
    iterate = system / scaling
    inverse_root = 1.5 * identity - 0.5 * iterate
    iterate = jnp.dot(iterate, inverse_root, precision=exact_precision)
    for iteration in range(1, SWEEPS):
        middle = 1.5 * identity - 0.5 * jnp.dot(inverse_root, iterate, precision=exact_precision)
        if iteration < SWEEPS - 1:
            iterate = jnp.dot(iterate, middle, precision=exact_precision)
        inverse_root = jnp.dot(middle, inverse_root, precision=exact_precision)
    forcing = jnp.broadcast_to(forcing, (members, SLOTS))
    inner = jnp.dot(inverse_root, forcing, precision=exact_precision)
    mean_weight = jnp.dot(inverse_root, inner, precision=exact_precision)[:, :1] / scaling
    weights = jnp.sqrt((members - 1) / scaling) * inverse_root + mean_weight
    weights = weights.T.astype(jnp.bfloat16)
    weights_ref[...] = weights

    own = members // (TURNS * DEPTHS)
    group = rows // own
    source_y = lax.rem(place_ref[0] + TURNS - group // DEPTHS, TURNS)
    source_z = lax.rem(place_ref[1] + DEPTHS - lax.rem(group, DEPTHS), DEPTHS)
    source = (source_y * DEPTHS + source_z) * own + lax.rem(rows, own)
    reorder = jnp.where(source == columns, 1.0, 0.0).astype(jnp.bfloat16)
    sided = lax.dot_general(
        weights, reorder, (((1,), (1,)), ((), ())), preferred_element_type=jnp.float32
    )
    sided_ref[...] = sided.astype(jnp.bfloat16)


def weights_for(listed, place, nears, others, pairs):
    members = nears[0].shape[0]
    vmem = pl.BlockSpec(memory_space=pltpu.VMEM)
    smem = pl.BlockSpec(memory_space=pltpu.SMEM)
    return pl.pallas_call(
        weights_kernel,
        in_specs=[smem, smem] + [vmem] * 9,
        out_specs=[vmem] * 2,
        out_shape=[jax.ShapeDtypeStruct((members, members), jnp.bfloat16)] * 2,
        scratch_shapes=[pltpu.VMEM((members, LISTED * SLOTS), jnp.bfloat16)],
        compiler_params=PARAMS,
        cost_estimate=WEIGHTS_COST,
    )(listed, place, *nears, *others, *pairs)


def turned_block(ref):
    return jnp.swapaxes(ref[...].reshape(ref.shape[0], *ref.shape[2:]).astype(jnp.float32), 0, 1)


def patch_at(place_ref, turn, depth):
    y = lax.rem(place_ref[0] + turn, TURNS)
    z = lax.rem(place_ref[1] + depth, DEPTHS)
    return y * DEPTHS + z


def pack_first_kernel(place_ref, fields_ref, *refs):
    out_refs, scratch = refs[:-1], refs[-1]
    scratch[...] = turned_block(fields_ref)
    for depth in range(DEPTHS):
        for turn in range(TURNS):
            block = scratch[patch_at(place_ref, turn, depth)]
            out_refs[depth][turn, 0] = block.astype(jnp.bfloat16)


def pack_first(place, fields, low, count):
    own, _, patches, columns = fields.shape
    return pl.pallas_call(
        pack_first_kernel,
        grid_spec=pltpu.PrefetchScalarGridSpec(
            num_scalar_prefetch=1,
            grid=(count,),
            in_specs=[pl.BlockSpec((own, 1, patches, columns), lambda v, s: (0, v + low, 0, 0))],
            out_specs=[
                pl.BlockSpec((TURNS, 1, own, columns), lambda v, s: (0, v, 0, 0))
                for _ in range(DEPTHS)
            ],
            scratch_shapes=[pltpu.VMEM((patches, own, columns), jnp.float32)],
        ),
        out_shape=[
            jax.ShapeDtypeStruct((TURNS, count, own, columns), fields.dtype) for _ in range(DEPTHS)
        ],
        compiler_params=PARAMS,
        cost_estimate=cost(own * count * patches * columns),
    )(place, fields)


def turn_kernel(fields_ref, out_ref):
    for level in range(fields_ref.shape[1]):
        out_ref[:, level] = jnp.swapaxes(fields_ref[:, level], 0, 1)


def turned(fields, low=0, params=PARAMS):
    outer, levels, inner, columns = fields.shape
    levels = levels - low
    return pl.pallas_call(
        turn_kernel,
        grid=(levels // STEP,),
        in_specs=[pl.BlockSpec((outer, STEP, inner, columns), lambda v: (0, v + low // STEP, 0, 0))],
        out_specs=pl.BlockSpec((inner, STEP, outer, columns), lambda v: (0, v, 0, 0)),
        out_shape=jax.ShapeDtypeStruct((inner, levels, outer, columns), fields.dtype),
        compiler_params=params,
        cost_estimate=cost(fields.size),
    )(fields)


def analyse(weights, wide):
    mean = jnp.sum(wide, axis=0, keepdims=True) * (1.0 / wide.shape[0])
    pert = (wide - mean).astype(jnp.bfloat16)
    return jnp.dot(weights, pert, preferred_element_type=jnp.float32) + mean


def apply_first_kernel(weights_ref, *refs):
    by_depth, by_turn, out_refs = refs[:8], refs[8:11], refs[11:]
    own, columns = by_depth[0].shape[2:]
    parts = [ref[0, 0].astype(jnp.float32) for ref in by_depth]
    for ref in by_turn:
        parts.append(ref[...].astype(jnp.float32).reshape(DEPTHS * own, columns))
    updated = analyse(weights_ref[...], jnp.concatenate(parts, axis=0))
    updated = updated.reshape(len(out_refs), TURNS * DEPTHS // len(out_refs), 1, own, columns)
    for part, ref in enumerate(out_refs):
        ref[...] = updated[part].astype(jnp.bfloat16)


def apply_first(weights, by_depth, by_turn, parts, levels):
    _, count, own, columns = by_depth[0].shape
    members = weights.shape[0]
    groups = TURNS * DEPTHS // parts
    taken = pl.BlockSpec((DEPTHS, 1, own, columns), lambda v: (0, v, 0, 0))
    given = pl.BlockSpec((groups, 1, own, columns), lambda v: (0, v, 0, 0))
    return pl.pallas_call(
        apply_first_kernel,
        grid=(count,),
        in_specs=[pl.BlockSpec((members, members), lambda v: (0, 0))]
        + [pl.BlockSpec((1, 1, own, columns), lambda v: (0, v, 0, 0))] * DEPTHS
        + [taken] * (TURNS - 1),
        out_specs=[given] * parts,
        out_shape=[jax.ShapeDtypeStruct((groups, levels, own, columns), jnp.bfloat16)] * parts,
        compiler_params=PARAMS,
        cost_estimate=cost(members * count * columns, 2 * members * members * count * columns),
    )(weights, *by_depth, *by_turn)


def apply_rest_kernel(weights_ref, fields_ref, _, out_ref):
    sources, levels, own, columns = fields_ref.shape
    for level in range(levels):
        wide = fields_ref[:, level].astype(jnp.float32).reshape(sources * own, columns)
        updated = analyse(weights_ref[...], wide).reshape(sources, own, columns)
        out_ref[:, level] = updated.astype(out_ref.dtype)


def apply_rest(weights, fields, whole):
    sources, levels, own, columns = fields.shape
    members = weights.shape[0]
    low = whole.shape[1] - levels
    return pl.pallas_call(
        apply_rest_kernel,
        grid=(levels // STEP,),
        in_specs=[
            pl.BlockSpec((members, members), lambda v: (0, 0)),
            pl.BlockSpec((sources, STEP, own, columns), lambda v: (0, v, 0, 0)),
            pl.BlockSpec(memory_space=pl.ANY),
        ],
        out_specs=pl.BlockSpec(
            (sources, STEP, own, columns), lambda v: (0, v + low // STEP, 0, 0)
        ),
        out_shape=jax.ShapeDtypeStruct(whole.shape, whole.dtype),
        input_output_aliases={2: 0},
        compiler_params=PARAMS,
        cost_estimate=cost(fields.size, 2 * members * fields.size),
    )(weights, fields, whole)


def observe(shaped_fields, where_flat, kernel):
    patch_count = where_flat.shape[0]
    slot_count = where_flat.shape[1]
    column_of = where_flat % COLUMNS
    variable_of = where_flat // COLUMNS
    column_iota = lax.broadcasted_iota(jnp.int32, (patch_count, COLUMNS, slot_count), 1)
    column_hot = (column_of[:, None, :] == column_iota).astype(jnp.bfloat16)
    spread = jnp.einsum(
        "kpvq,pqo->kpvo", shaped_fields, column_hot, preferred_element_type=jnp.float32
    )
    variable_iota = lax.broadcasted_iota(jnp.int32, (patch_count, VARIABLES, slot_count), 1)
    variable_weight = jnp.where(
        variable_of[:, None, :] == variable_iota, kernel[None, :, None], 0.0
    )
    return jnp.sum(spread * variable_weight[None], axis=2)


def body(ensemble, observations, precision, valid_count, position, level_kernel, listed_blocks):
    kernel = level_kernel[0]
    own = ensemble.shape[0]
    row_patches = ensemble.shape[2]
    members = own * row_patches
    fields = ensemble.reshape(own, row_patches, VARIABLES, COLUMNS)
    turned_fields = fields.transpose(0, 2, 1, 3)
    here = lax.axis_index("member")
    level = lax.axis_index("level")
    place = jnp.stack([here // DEPTHS, here % DEPTHS, level]).astype(jnp.int32)

    slot_index = lax.broadcasted_iota(jnp.int32, precision.shape, 3)
    precision_used = jnp.where(slot_index < valid_count[..., None], precision, 0.0)
    table = jnp.concatenate(
        [
            position.reshape(OWN_BLOCKS, SLOTS).astype(jnp.float32),
            observations.reshape(OWN_BLOCKS, SLOTS),
            precision_used.reshape(OWN_BLOCKS, SLOTS),
        ]
    )
    tables = exchange(jnp.broadcast_to(table[None], (row_patches,) + table.shape))

    packed = pack_first(place, turned_fields, 0, FIRST)
    by_depth = [packed[0]] + [shifted(packed[depth], 0, depth) for depth in range(1, DEPTHS)]

    where = tables[:, :OWN_BLOCKS].reshape(row_patches, OWN_BLOCKS * SLOTS).astype(jnp.int32)
    level_term = observe(fields, where, kernel)
    equivalent = lax.psum(level_term, "level").astype(jnp.bfloat16)
    equivalent = jnp.where(level == 0, equivalent[:, :, :SLOTS], equivalent[:, :, SLOTS:])
    padded = jnp.pad(equivalent, ((0, 0), (1, 1), (0, 0)))
    spread = jnp.concatenate(
        [padded[:, shift : shift + row_patches] for shift in range(3)], axis=2
    ).transpose(1, 0, 2)
    spread, by_depth[1], by_depth[7], by_depth[2], by_depth[6], by_depth[4] = barrier(
        (spread, by_depth[1], by_depth[7], by_depth[2], by_depth[6], by_depth[4])
    )
    near = exchange(spread).reshape(members, 3 * SLOTS)

    outgoing = turned(turned_fields, FIRST)
    outgoing, near, by_depth[3], by_depth[5] = barrier(
        (outgoing, near, by_depth[3], by_depth[5])
    )
    incoming = exchange(outgoing)
    by_turn = [
        shifted(jnp.stack([piece[turn] for piece in by_depth]), turn, 0)
        for turn in range(1, TURNS)
    ]

    pair_rows = jnp.pad(tables[:, OWN_BLOCKS:], ((1, 1), (0, 0), (0, 0)))
    pair_own = lax.dynamic_slice_in_dim(pair_rows, here, 3, axis=0)
    pair_above, pair_below = row_halo(pair_own)
    near_above, near_below = row_halo(near)
    nears = [near_above, near, near_below]
    weights, sided = weights_for(
        listed_blocks[0, 0],
        place,
        nears,
        [swapped(cells) for cells in nears],
        [pair_above, pair_own, pair_below],
    )
    outs = apply_first(sided, by_depth, by_turn, 1, VARIABLES)[0]
    incoming, outs = barrier((incoming, outs))
    outs = apply_rest(weights, incoming, outs)
    whole = turned(exchange(outs), params=SMALL)
    return whole.transpose(0, 2, 1, 3).reshape(ensemble.shape)


def solution(mesh):
    placed = (
        P("member", "patch", None, "level", None, None),
        P("patch", "member", None, None),
        P("patch", "member", None, None),
        P("patch", "member", None),
        P("patch", "member", None, None),
        P("level", None),
        P("patch", "member", None),
    )
    return jax.shard_map(
        body,
        mesh=mesh,
        in_specs=placed,
        out_specs=P("member", "patch", None, "level", None, None),
        check_vma=False,
    )
```

time: 370 us -> 347 us (0.938)
  waiting for transfers between devices: 116 us -> 76 us
  blocking collectives: 127 us -> 152 us
  Pallas kernels: 9.94 us -> 34 us
  local copies, waits for them, and re-layouts: 27.6 us -> 7.46 us
  between operations: 16.4 us -> 0.34 us
  starting transfers between devices: 48.2 us -> 61.9 us
  matrix products: 19.2 us -> 10.7 us
    all_to_all x5 -> x3, waiting for transfers between devices: 116 us -> 33 us  [exchange(): lax.all_to_all(cells, 'member', split_axis=0, concat_axis=0, tiled=True)]
    ppermute x0 -> x13, waiting for transfers between devices: none -> 30.9 us  [the longest x10 29.5 us: shifted(): return lax.ppermute(cells, 'member', pairs)]
    all_to_all x1, blocking collectives: 123 us -> 148 us  [exchange(): lax.all_to_all(cells, 'member', split_axis=0, concat_axis=0, tiled=True)]
    pallas_call x2 -> x6, Pallas kernels: 9.94 us -> 34 us  [the longest x1 10.5 us: weights_for(): pl.pallas_call(weights_kernel, in_specs=[smem, smem] + [vmem] * 9, out_sp...]
    ppermute x0 -> x13, starting transfers between devices: none -> 22.9 us  [the longest x10 22.9 us: shifted(): return lax.ppermute(cells, 'member', pairs)]
    ppermute x2, waiting for transfers between devices: 0.01 us -> 8.91 us  [row_halo(): above = lax.ppermute(cells, 'patch', [(i, i + 1) for i in range(count - 1)])]
    dot_general x22 -> x0, matrix products: 8.55 us -> none  [the longest x6 2.22 us: weights_for(): jnp.dot(inverse_root, iterate, precision=exact_precision)]
    all_to_all x5 -> x3, starting transfers between devices: 38.1 us -> 29.8 us  [exchange(): lax.all_to_all(cells, 'member', split_axis=0, concat_axis=0, tiled=True)]
  transfers between devices with their start and end apart: 9 -> 20, of which waited for: 5 -> 10; matrix products, arithmetic and copies ran while one was open for 10% -> 5% of each run, Pallas kernels for 3% -> 7%
where the time goes in v2:
time: 347 us; the launch traced here: 346 us
  blocking collectives  152 us (44%)
  waiting for transfers between devices  76 us (22%)
  starting transfers between devices  61.9 us (18%)
  Pallas kernels  34 us (10%)
  matrix products  10.7 us (3%)
  local copies, waits for them, and re-layouts  7.46 us (2%)
  other arithmetic  3.62 us (1%)
    all_to_all x1, blocking collectives, exchange(): lax.all_to_all(cells, 'member', split_axis=0, concat_axis=0, tiled=True)  148 us
    all_to_all x3, waiting for transfers between devices, exchange(): lax.all_to_all(cells, 'member', split_axis=0, concat_axis=0, tiled=True)  33 us
    all_to_all x3, starting transfers between devices, exchange(): lax.all_to_all(cells, 'member', split_axis=0, concat_axis=0, tiled=True)  29.8 us
    ppermute x10, waiting for transfers between devices, shifted(): return lax.ppermute(cells, 'member', pairs)  29.5 us
    ppermute x10, starting transfers between devices, shifted(): return lax.ppermute(cells, 'member', pairs)  22.9 us
    dot_general x1, matrix products, observe(): jnp.einsum('kpvq,pqo->kpvo', shaped_fields, column_hot, preferred_element...  10.7 us
    pallas_call x1, Pallas kernels, weights_for(): pl.pallas_call(weights_kernel, in_specs=[smem, smem] + [vmem] * 9, out_sp...  10.5 us
    ppermute x2, waiting for transfers between devices, row_halo(): above = lax.ppermute(cells, 'patch', [(i, i + 1) for i in range(count - 1)])  8.91 us
  transfers between devices with their start and end apart: 20, of which 10 were waited for; matrix products, arithmetic and copies ran while one was open for 5% of the time, Pallas kernels for 7%

profile of v2, /device:TPU:6, one launch (start us, length us, event | category | flops | bytes accessed | tf_op | source)
XLA Modules:
  0.0 346.1 jit_solution(10844907885895946822)
XLA Ops:
  2.8 11.5 %all-to-all-start = ((f32[32,6,128]{2,1,0:T(8,128)}), f32[32,6,128]{2,1,0:T(8,128)S(1)}, u32[]{:S(2)}, u32[]{:S(2)}) async-start(f32[32,6,128]{2,1,0:T(8,128)} %broadcast_in_dim.29), calls=%async_computation | async-start | bytes 262144 | tf_op jit(solution)/shard_map/all_to_all | solution.py:24
  14.9 4.9 %shard_map.77 = (bf16[4,4,8,1024]{3,2,1,0:T(8,128)(2,1)}, bf16[4,4,8,1024]{3,2,1,0:T(8,128)(2,1)}, bf16[4,4,8,1024]{3,2,1,0:T(8,128)(2,1)}, bf16[4,4,8,1024]{3,2...) custom-call(s32[3]{0:T(128)} %pad_add_fusion.place_ref, ...), custom_call_target="tpu_custom_call" | custom-call | bytes 4194304 | tf_op jit(solution)/shard_map/pallas_call | solution.py:162
  24.6 2.7 collective-permute-start.3
  27.2 5.7 %collective-permute-start.4 = (bf16[4,4,8,1024]{3,2,1,0:T(8,128)(2,1)}, bf16[4,4,8,1024]{3,2,1,0:T(8,128)(2,1)S(1)}, u32[]{:S(2)}, u32[]{:S(2)}) collective-permute-start(bf16[4,4,8,1024]{3,2,1,0:T(8,128)(2,1)} %get-tuple-element.31), channel_id=1, source_target_pairs={{0,32},{8,40},{16,48},{24,56},{32,0},{40,8},{48,16},{56,24},{64,96... | collective-permute-start | bytes 786440 | tf_op jit(solution)/shard_map/ppermute | solution.py:39
  33.1 10.7 %fusion.5 = f32[8,32,256]{2,0,1:T(8,128)S(1)} fusion(bf16[8,32,12,1024]{3,1,2,0:T(8,128)(2,1)} %bitcast.61, s32[32,256]{1,0:T(8,128)S(1)} %get-tuple-element.76, f32[32,12,256]{2,1,0:T(8,128)S(1)} %fusion.10), kind=kOutput, calls=%fused_computation.6 | convolution fusion | flops 1620508672 | bytes 6979584 | tf_op jit(solution)/shard_map/kpvq,pqo->kpvo/dot_general | solution.py:275
  43.9 4.2 %all-reduce.3 = bf16[8,32,256]{2,0,1:T(8,128)(2,1)S(1)} all-reduce(f32[8,32,256]{2,0,1:T(8,128)S(1)} %fusion.5), channel_id=1, replica_groups=mesh['member'=32,'patch'=4,'level'=2] {'level'}, use_global_device_ids=true, to_apply=%region_1.2 | all-reduce | flops 65536 | bytes 393216 | tf_op jit(solution)/shard_map/psum | solution.py:312
  50.9 10.4 %all-to-all-start.1 = ((bf16[32,8,384]{2,1,0:T(8,128)(2,1)}), bf16[32,8,384]{2,1,0:T(8,128)(2,1)S(1)}, u32[]{:S(2)}, u32[]{:S(2)}) async-start(bf16[32,8,384]{2,1,0:T(8,128)(2,1)} %maximum_bitcast_fusion), calls=%async_computation.1 | async-start | bytes 393216 | tf_op jit(solution)/shard_map/all_to_all | solution.py:24
  61.3 3.7 %collective-permute-start.5 = (bf16[4,4,8,1024]{3,2,1,0:T(8,128)(2,1)S(1)}, bf16[4,4,8,1024]{3,2,1,0:T(8,128)(2,1)S(1)}, u32[]{:S(2)}, u32[]{:S(2)}) collective-permute-start(bf16[4,4,8,1024]{3,2,1,0:T(8,128)(2,1)S(1)} %copy-done.22), channel_id=1, source_target_pairs={{0,24},{8,32},{16,40},{24,48},{32,56},{40,0},{48,8},{56,16},{64,88... | collective-permute-start | bytes 786440 | tf_op jit(solution)/shard_map/ppermute | solution.py:39
  66.5 4.1 %shard_map.76 = bf16[32,8,8,1024]{3,2,1,0:T(8,128)(2,1)} custom-call(bf16[8,12,32,1024]{3,2,1,0:T(8,128)(2,1)} %bitcast.62), custom_call_target="tpu_custom_call" | custom-call | bytes 12582912 | tf_op jit(solution)/shard_map/pallas_call | solution.py:190
  70.6 13.9 %collective-permute-done.5.refs_3_ = bf16[4,4,8,1024]{3,2,1,0:T(8,128)(2,1)S(1)} collective-permute-done((bf16[4,4,8,1024]{3,2,1,0:T(8,128)(2,1)S(1)}, bf16[4,4,8,1024]{3,2,1,0:T(8,128)(2,1)S(1)}, u32[]{:S(2)}, u32[]{:S(2)}) %collective-permute-start.5) | collective-permute-done | bytes 262176 | tf_op jit(solution)/shard_map/ppermute | solution.py:39
  84.5 7.9 %all-to-all-start.2 = ((bf16[32,8,8,1024]{3,2,1,0:T(8,128)(2,1)}), bf16[32,8,8,1024]{3,2,1,0:T(8,128)(2,1)}, u32[]{:S(2)}, u32[]{:S(2)}) async-start(bf16[32,8,8,1024]{3,2,1,0:T(8,128)(2,1)} %shard_map.76), calls=%async_computation.2 | async-start | bytes 8388608 | tf_op jit(solution)/shard_map/all_to_all | solution.py:24
  97.7 3.0 collective-permute-start.16
  102.4 2.7 collective-permute-start.13
  107.7 4.5 %collective-permute-done.12.refs_6_ = f32[3,4,128]{2,1,0:T(4,128)S(1)} collective-permute-done((f32[3,4,128]{2,1,0:T(4,128)S(1)}, f32[3,4,128]{2,1,0:T(4,128)S(1)}, u32[]{:S(2)}, u32[]{:S(2)}) %collective-permute-start.12) | collective-permute-done | bytes 6176 | tf_op jit(solution)/shard_map/ppermute | solution.py:29
  112.2 3.9 %collective-permute-start.8 = (bf16[256,384]{1,0:T(8,128)(2,1)S(1)}, bf16[256,384]{1,0:T(8,128)(2,1)S(1)}, u32[]{:S(2)}, u32[]{:S(2)}) collective-permute-start(bf16[256,384]{1,0:T(8,128)(2,1)S(1)} %bitcast.64), channel_id=1, source_target_pairs={{2,0},{4,2},{6,4},{3,1},{5,3},{7,5},{10,8},{12,10},{14,12},{11,9},... | collective-permute-start | bytes 589832 | tf_op jit(solution)/shard_map/ppermute | solution.py:30
  119.3 4.4 %collective-permute-done.7.refs_0_ = bf16[256,384]{1,0:T(8,128)(2,1)S(1)} collective-permute-done((bf16[256,384]{1,0:T(8,128)(2,1)S(1)}, bf16[256,384]{1,0:T(8,128)(2,1)S(1)}, u32[]{:S(2)}, u32[]{:S(2)}) %collective-permute-start.7) | collective-permute-done | bytes 196640 | tf_op jit(solution)/shard_map/ppermute | solution.py:29
  125.9 10.5 %shard_map.78 = (bf16[256,256]{1,0:T(8,128)(2,1)}, bf16[256,256]{1,0:T(8,128)(2,1)}) custom-call(s32[8]{0:T(128)} %bitcast.70, s32[3]{0:T(128)} %pad_add_fusion.place_ref, bf16[256,384]{1,0:T(8,128)(2,1)} %copy-done.14, bf16[256,384]{1,0:T(8,128)(2,1)} %bitcast.66, bf16[256,384]{1,0:T(8,128)(2,1)} %copy-done.13, bf16[256,384]{1,0:T(8,128)(2,1)} %copy-done.16, ...), custom_call_target="tpu_custom_call" | custom-call | bytes 1024 | tf_op jit(solution)/shard_map/pallas_call | solution.py:130
  136.4 4.7 %collective-permute-done.16.refs_10_ = bf16[8,4,8,1024]{3,2,1,0:T(8,128)(2,1)S(1)} collective-permute-done((bf16[8,4,8,1024]{3,2,1,0:T(8,128)(2,1)S(1)}, bf16[8,4,8,1024]{3,2,1,0:T(8,128)(2,1)S(1)}, u32[]{:S(2)}, u32[]{:S(2)}) %collective-permute-start.16) | collective-permute-done | bytes 524320 | tf_op jit(solution)/shard_map/ppermute | solution.py:39
  141.1 8.8 %collective-permute-done.14.refs_8_ = bf16[8,4,8,1024]{3,2,1,0:T(8,128)(2,1)S(1)} collective-permute-done((bf16[8,4,8,1024]{3,2,1,0:T(8,128)(2,1)}, bf16[8,4,8,1024]{3,2,1,0:T(8,128)(2,1)S(1)}, u32[]{:S(2)}, u32[]{:S(2)}) %collective-permute-start.14) | collective-permute-done | bytes 524320 | tf_op jit(solution)/shard_map/ppermute | solution.py:39
  150.7 4.9 %shard_map.79._ = bf16[32,12,8,1024]{3,2,1,0:T(8,128)(2,1)} custom-call(bf16[256,256]{1,0:T(8,128)(2,1)} %get-tuple-element.38.weights_ref, bf16[4,4,8,1024]{3,2,1,0:T(8,128)(2,1)} %get-tuple-element.39.refs_0_, bf16[4,4,8,1024]{3,2,1,0:T(8,128)(2,1)} %copy-done.1, bf16[4,4,8,1024]{3,2,1,0:T(8,128)(2,1)} %copy-done.3, bf16[4,4,8,1024]{3,2,1,0:T(8,128)(2,1)} %copy-done.6, ...), custom_call_target="tpu_custom_call" | custom-call | flops 536870912 | bytes 4194304 | tf_op jit(solution)/shard_map/pallas_call | solution.py:225
  155.7 33.0 %all-to-all-done.2.fields_ref = bf16[32,8,8,1024]{3,2,1,0:T(8,128)(2,1)} async-done(((bf16[32,8,8,1024]{3,2,1,0:T(8,128)(2,1)}), bf16[32,8,8,1024]{3,2,1,0:T(8,128)(2,1)}, u32[]{:S(2)}, u32[]{:S(2)}) %all-to-all-start.2) | async-done | bytes 4194336 | tf_op jit(solution)/shard_map/all_to_all | solution.py:24
  188.6 5.6 %shard_map.80 = bf16[32,12,8,1024]{3,2,1,0:T(8,128)(2,1)} custom-call(bf16[256,256]{1,0:T(8,128)(2,1)} %get-tuple-element.36.weights_ref, bf16[32,8,8,1024]{3,2,1,0:T(8,128)(2,1)} %all-to-all-done.2.fields_ref, bf16[32,12,8,1024]{3,2,1,0:T(8,128)(2,1)} %shard_map.79._), custom_call_target="tpu_custom_call", output_to_operand_aliasing={{}: (2, {})} | custom-call | flops 1073741824 | bytes 8388608 | tf_op jit(solution)/shard_map/pallas_call | solution.py:250
  194.2 147.9 %all_to_all.20.fields_ref = bf16[32,12,8,1024]{3,2,1,0:T(8,128)(2,1)S(1)} all-to-all(bf16[32,12,8,1024]{3,2,1,0:T(8,128)(2,1)} %shard_map.80), channel_id=1, replica_groups=mesh['member'=32,'patch'=4,'level'=2] {'member'}, dimensions={0} | all-to-all | bytes 12582912 | tf_op jit(solution)/shard_map/all_to_all | solution.py:24
  342.2 4.0 %shard_map.81 = bf16[8,12,32,1024]{3,2,1,0:T(8,128)(2,1)} custom-call(bf16[32,12,8,1024]{3,2,1,0:T(8,128)(2,1)S(1)} %all_to_all.20.fields_ref), custom_call_target="tpu_custom_call" | custom-call | bytes 12582912 | tf_op jit(solution)/shard_map/pallas_call | solution.py:190
  (92 shorter events, 28.2 us)
Async XLA Ops:
  2.8 30.1 %all-to-all-start = ((f32[32,6,128]{2,1,0:T(8,128)}), f32[32,6,128]{2,1,0:T(8,128)S(1)}, u32[]{:S(2)}, u32[]{:S(2)}) async-start(f32[32,6,128]{2,1,0:T(8,128)} %broadcast_in_dim.29), calls=%async_computation | async-start | bytes 262144 | tf_op jit(solution)/shard_map/all_to_all | solution.py:24
  19.8 29.0 %collective-permute-start = (bf16[4,4,8,1024]{3,2,1,0:T(8,128)(2,1)}, bf16[4,4,8,1024]{3,2,1,0:T(8,128)(2,1)S(1)}, u32[]{:S(2)}, u32[]{:S(2)}) collective-permute-start(bf16[4,4,8,1024]{3,2,1,0:T(8,128)(2,1)} %get-tuple-element.27), channel_id=1, source_target_pairs={{0,8},{8,16},{16,24},{24,32},{32,40},{40,48},{48,56},{56,0},{64,72... | collective-permute-start | bytes 786440 | tf_op jit(solution)/shard_map/ppermute | solution.py:39
  21.6 27.2 %collective-permute-start.1 = (bf16[4,4,8,1024]{3,2,1,0:T(8,128)(2,1)}, bf16[4,4,8,1024]{3,2,1,0:T(8,128)(2,1)S(1)}, u32[]{:S(2)}, u32[]{:S(2)}) collective-permute-start(bf16[4,4,8,1024]{3,2,1,0:T(8,128)(2,1)} %get-tuple-element.28), channel_id=1, source_target_pairs={{0,56},{8,0},{16,8},{24,16},{32,24},{40,32},{48,40},{56,48},{64,12... | collective-permute-start | bytes 786440 | tf_op jit(solution)/shard_map/ppermute | solution.py:39
  23.1 25.8 %collective-permute-start.2 = (bf16[4,4,8,1024]{3,2,1,0:T(8,128)(2,1)}, bf16[4,4,8,1024]{3,2,1,0:T(8,128)(2,1)S(1)}, u32[]{:S(2)}, u32[]{:S(2)}) collective-permute-start(bf16[4,4,8,1024]{3,2,1,0:T(8,128)(2,1)} %get-tuple-element.29), channel_id=1, source_target_pairs={{0,16},{8,24},{16,32},{24,40},{32,48},{40,56},{48,0},{56,8},{64,80... | collective-permute-start | bytes 786440 | tf_op jit(solution)/shard_map/ppermute | solution.py:39
  24.6 26.3 %collective-permute-start.3 = (bf16[4,4,8,1024]{3,2,1,0:T(8,128)(2,1)}, bf16[4,4,8,1024]{3,2,1,0:T(8,128)(2,1)S(1)}, u32[]{:S(2)}, u32[]{:S(2)}) collective-permute-start(bf16[4,4,8,1024]{3,2,1,0:T(8,128)(2,1)} %get-tuple-element.30), channel_id=1, source_target_pairs={{0,48},{8,56},{16,0},{24,8},{32,16},{40,24},{48,32},{56,40},{64,11... | collective-permute-start | bytes 786440 | tf_op jit(solution)/shard_map/ppermute | solution.py:39
  27.2 23.7 %collective-permute-start.4 = (bf16[4,4,8,1024]{3,2,1,0:T(8,128)(2,1)}, bf16[4,4,8,1024]{3,2,1,0:T(8,128)(2,1)S(1)}, u32[]{:S(2)}, u32[]{:S(2)}) collective-permute-start(bf16[4,4,8,1024]{3,2,1,0:T(8,128)(2,1)} %get-tuple-element.31), channel_id=1, source_target_pairs={{0,32},{8,40},{16,48},{24,56},{32,0},{40,8},{48,16},{56,24},{64,96... | collective-permute-start | bytes 786440 | tf_op jit(solution)/shard_map/ppermute | solution.py:39
  48.8 48.2 %copy-start.2 = (bf16[4,4,8,1024]{3,2,1,0:T(8,128)(2,1)}, bf16[4,4,8,1024]{3,2,1,0:T(8,128)(2,1)S(1)}, u32[]{:S(2)}) copy-start(bf16[4,4,8,1024]{3,2,1,0:T(8,128)(2,1)S(1)} %collective-permute-done.1.refs_7_) | copy-start | bytes 786436
  50.9 45.5 %copy-start.4 = (bf16[4,4,8,1024]{3,2,1,0:T(8,128)(2,1)}, bf16[4,4,8,1024]{3,2,1,0:T(8,128)(2,1)S(1)}, u32[]{:S(2)}) copy-start(bf16[4,4,8,1024]{3,2,1,0:T(8,128)(2,1)S(1)} %collective-permute-done.3.refs_6_) | copy-start | bytes 786436
  50.9 33.6 %all-to-all-start.1 = ((bf16[32,8,384]{2,1,0:T(8,128)(2,1)}), bf16[32,8,384]{2,1,0:T(8,128)(2,1)S(1)}, u32[]{:S(2)}, u32[]{:S(2)}) async-start(bf16[32,8,384]{2,1,0:T(8,128)(2,1)} %maximum_bitcast_fusion), calls=%async_computation.1 | async-start | bytes 393216 | tf_op jit(solution)/shard_map/all_to_all | solution.py:24
  61.3 23.1 %collective-permute-start.5 = (bf16[4,4,8,1024]{3,2,1,0:T(8,128)(2,1)S(1)}, bf16[4,4,8,1024]{3,2,1,0:T(8,128)(2,1)S(1)}, u32[]{:S(2)}, u32[]{:S(2)}) collective-permute-start(bf16[4,4,8,1024]{3,2,1,0:T(8,128)(2,1)S(1)} %copy-done.22), channel_id=1, source_target_pairs={{0,24},{8,32},{16,40},{24,48},{32,56},{40,0},{48,8},{56,16},{64,88... | collective-permute-start | bytes 786440 | tf_op jit(solution)/shard_map/ppermute | solution.py:39
  65.0 19.5 %collective-permute-start.6 = (bf16[4,4,8,1024]{3,2,1,0:T(8,128)(2,1)S(1)}, bf16[4,4,8,1024]{3,2,1,0:T(8,128)(2,1)S(1)}, u32[]{:S(2)}, u32[]{:S(2)}) collective-permute-start(bf16[4,4,8,1024]{3,2,1,0:T(8,128)(2,1)S(1)} %copy-done.21), channel_id=1, source_target_pairs={{0,40},{8,48},{16,56},{24,0},{32,8},{40,16},{48,24},{56,32},{64,10... | collective-permute-start | bytes 786440 | tf_op jit(solution)/shard_map/ppermute | solution.py:39
  84.5 51.9 %copy-start.6 = (bf16[4,4,8,1024]{3,2,1,0:T(8,128)(2,1)}, bf16[4,4,8,1024]{3,2,1,0:T(8,128)(2,1)S(1)}, u32[]{:S(2)}) copy-start(bf16[4,4,8,1024]{3,2,1,0:T(8,128)(2,1)S(1)} %collective-permute-done.5.refs_3_) | copy-start | bytes 786436
  84.5 51.9 %copy-start.7 = (bf16[4,4,8,1024]{3,2,1,0:T(8,128)(2,1)}, bf16[4,4,8,1024]{3,2,1,0:T(8,128)(2,1)S(1)}, u32[]{:S(2)}) copy-start(bf16[4,4,8,1024]{3,2,1,0:T(8,128)(2,1)S(1)} %collective-permute-done.6.refs_5_) | copy-start | bytes 786436
  84.5 104.1 %all-to-all-start.2 = ((bf16[32,8,8,1024]{3,2,1,0:T(8,128)(2,1)}), bf16[32,8,8,1024]{3,2,1,0:T(8,128)(2,1)}, u32[]{:S(2)}, u32[]{:S(2)}) async-start(bf16[32,8,8,1024]{3,2,1,0:T(8,128)(2,1)} %shard_map.76), calls=%async_computation.2 | async-start | bytes 8388608 | tf_op jit(solution)/shard_map/all_to_all | solution.py:24
  94.4 21.8 %collective-permute-start.10 = (bf16[256,384]{1,0:T(8,128)(2,1)S(1)}, bf16[256,384]{1,0:T(8,128)(2,1)S(1)}, u32[]{:S(2)}, u32[]{:S(2)}) collective-permute-start(bf16[256,384]{1,0:T(8,128)(2,1)S(1)} %bitcast.63), channel_id=1, source_target_pairs={{0,1},{1,0},{2,3},{3,2},{4,5},{5,4},{6,7},{7,6},{8,9},{9,8},{10,11... | collective-permute-start | bytes 589832 | tf_op jit(solution)/shard_map/ppermute | solution.py:43
  97.7 43.4 %collective-permute-start.16 = (bf16[8,4,8,1024]{3,2,1,0:T(8,128)(2,1)S(1)}, bf16[8,4,8,1024]{3,2,1,0:T(8,128)(2,1)S(1)}, u32[]{:S(2)}, u32[]{:S(2)}) collective-permute-start(bf16[8,4,8,1024]{3,2,1,0:T(8,128)(2,1)S(1)} %get-tuple-element.49), channel_id=1, source_target_pairs={{0,192},{8,200},{16,208},{24,216},{32,224},{40,232},{48,240},{56,2... | collective-permute-start | bytes 1572872 | tf_op jit(solution)/shard_map/ppermute | solution.py:39
  100.6 40.4 %collective-permute-start.15 = (bf16[8,4,8,1024]{3,2,1,0:T(8,128)(2,1)}, bf16[8,4,8,1024]{3,2,1,0:T(8,128)(2,1)S(1)}, u32[]{:S(2)}, u32[]{:S(2)}) collective-permute-start(bf16[8,4,8,1024]{3,2,1,0:T(8,128)(2,1)} %get-tuple-element.50), channel_id=1, source_target_pairs={{0,128},{8,136},{16,144},{24,152},{32,160},{40,168},{48,176},{56,1... | collective-permute-start | bytes 1572872 | tf_op jit(solution)/shard_map/ppermute | solution.py:39
  101.5 48.4 %collective-permute-start.14 = (bf16[8,4,8,1024]{3,2,1,0:T(8,128)(2,1)}, bf16[8,4,8,1024]{3,2,1,0:T(8,128)(2,1)S(1)}, u32[]{:S(2)}, u32[]{:S(2)}) collective-permute-start(bf16[8,4,8,1024]{3,2,1,0:T(8,128)(2,1)} %get-tuple-element.51), channel_id=1, source_target_pairs={{0,64},{8,72},{16,80},{24,88},{32,96},{40,104},{48,112},{56,120},{... | collective-permute-start | bytes 1572872 | tf_op jit(solution)/shard_map/ppermute | solution.py:39
  102.4 4.1 %collective-permute-start.13 = (f32[3,4,128]{2,1,0:T(4,128)S(1)}, f32[3,4,128]{2,1,0:T(4,128)S(1)}, u32[]{:S(2)}, u32[]{:S(2)}) collective-permute-start(f32[3,4,128]{2,1,0:T(4,128)S(1)} %pad_dynamic-slice_fusion.refs_7_), channel_id=1, source_target_pairs={{2,0},{4,2},{6,4},{3,1},{5,3},{7,5},{10,8},{12,10},{14,12},{11,9},... | collective-permute-start | bytes 18440 | tf_op jit(solution)/shard_map/ppermute | solution.py:30
  106.5 5.8 %collective-permute-start.12 = (f32[3,4,128]{2,1,0:T(4,128)S(1)}, f32[3,4,128]{2,1,0:T(4,128)S(1)}, u32[]{:S(2)}, u32[]{:S(2)}) collective-permute-start(f32[3,4,128]{2,1,0:T(4,128)S(1)} %pad_dynamic-slice_fusion.refs_7_), channel_id=1, source_target_pairs={{0,2},{2,4},{4,6},{1,3},{3,5},{5,7},{8,10},{10,12},{12,14},{9,11},... | collective-permute-start | bytes 18440 | tf_op jit(solution)/shard_map/ppermute | solution.py:29
  112.2 7.1 %collective-permute-start.8 = (bf16[256,384]{1,0:T(8,128)(2,1)S(1)}, bf16[256,384]{1,0:T(8,128)(2,1)S(1)}, u32[]{:S(2)}, u32[]{:S(2)}) collective-permute-start(bf16[256,384]{1,0:T(8,128)(2,1)S(1)} %bitcast.64), channel_id=1, source_target_pairs={{2,0},{4,2},{6,4},{3,1},{5,3},{7,5},{10,8},{12,10},{14,12},{11,9},... | collective-permute-start | bytes 589832 | tf_op jit(solution)/shard_map/ppermute | solution.py:30
  116.2 7.6 %collective-permute-start.7 = (bf16[256,384]{1,0:T(8,128)(2,1)S(1)}, bf16[256,384]{1,0:T(8,128)(2,1)S(1)}, u32[]{:S(2)}, u32[]{:S(2)}) collective-permute-start(bf16[256,384]{1,0:T(8,128)(2,1)S(1)} %bitcast.65), channel_id=1, source_target_pairs={{0,2},{2,4},{4,6},{1,3},{3,5},{5,7},{8,10},{10,12},{12,14},{9,11},... | collective-permute-start | bytes 589832 | tf_op jit(solution)/shard_map/ppermute | solution.py:29
  119.3 4.4 %collective-permute-start.11 = (bf16[256,384]{1,0:T(8,128)(2,1)S(1)}, bf16[256,384]{1,0:T(8,128)(2,1)S(1)}, u32[]{:S(2)}, u32[]{:S(2)}) collective-permute-start(bf16[256,384]{1,0:T(8,128)(2,1)S(1)} %collective-permute-done.8.refs_2_), channel_id=1, source_target_pairs={{0,1},{1,0},{2,3},{3,2},{4,5},{5,4},{6,7},{7,6},{8,9},{9,8},{10,11... | collective-permute-start | bytes 589832 | tf_op jit(solution)/shard_map/ppermute | solution.py:43
  123.8 1.4 collective-permute-start.9
  (19 other events, 380.5 us)

commit v3 on v2

--- a/solution.py
+++ b/solution.py
@@ -13,6 +13,7 @@
 SWEEPS = 6
 FIRST = 4
 STEP = 4
+PAIR = 2
 DEPTHS = 8
 TURNS = 4
 
@@ -138,10 +139,6 @@
     )(listed, place, *nears, *others, *pairs)
 
 
-def turned_block(ref):
-    return jnp.swapaxes(ref[...].reshape(ref.shape[0], *ref.shape[2:]).astype(jnp.float32), 0, 1)
-
-
 def patch_at(place_ref, turn, depth):
     y = lax.rem(place_ref[0] + turn, TURNS)
     z = lax.rem(place_ref[1] + depth, DEPTHS)
@@ -150,26 +147,26 @@
 
 def pack_first_kernel(place_ref, fields_ref, *refs):
     out_refs, scratch = refs[:-1], refs[-1]
-    scratch[...] = turned_block(fields_ref)
-    for depth in range(DEPTHS):
-        for turn in range(TURNS):
-            block = scratch[patch_at(place_ref, turn, depth)]
-            out_refs[depth][turn, 0] = block.astype(jnp.bfloat16)
-
-
-def pack_first(place, fields, low, count):
+    for level in range(PAIR):
+        scratch[...] = jnp.swapaxes(fields_ref[:, level], 0, 1)
+        for depth in range(DEPTHS):
+            for turn in range(TURNS):
+                out_refs[depth][turn, level] = scratch[patch_at(place_ref, turn, depth)]
+
+
+def pack_first(place, fields, count):
     own, _, patches, columns = fields.shape
     return pl.pallas_call(
         pack_first_kernel,
         grid_spec=pltpu.PrefetchScalarGridSpec(
             num_scalar_prefetch=1,
-            grid=(count,),
-            in_specs=[pl.BlockSpec((own, 1, patches, columns), lambda v, s: (0, v + low, 0, 0))],
+            grid=(count // PAIR,),
+            in_specs=[pl.BlockSpec((own, PAIR, patches, columns), lambda v, s: (0, v, 0, 0))],
             out_specs=[
-                pl.BlockSpec((TURNS, 1, own, columns), lambda v, s: (0, v, 0, 0))
+                pl.BlockSpec((TURNS, PAIR, own, columns), lambda v, s: (0, v, 0, 0))
                 for _ in range(DEPTHS)
             ],
-            scratch_shapes=[pltpu.VMEM((patches, own, columns), jnp.float32)],
+            scratch_shapes=[pltpu.VMEM((patches, own, columns), fields.dtype)],
         ),
         out_shape=[
             jax.ShapeDtypeStruct((TURNS, count, own, columns), fields.dtype) for _ in range(DEPTHS)
@@ -177,6 +174,28 @@
         compiler_params=PARAMS,
         cost_estimate=cost(own * count * patches * columns),
     )(place, fields)
+
+
+def table_kernel(count_ref, position_ref, observed_ref, precision_ref, out_ref):
+    slot = lax.broadcasted_iota(jnp.int32, (1, SLOTS), 1)
+    used = [
+        jnp.where(slot < count_ref[block], precision_ref[block : block + 1], 0.0)
+        for block in range(OWN_BLOCKS)
+    ]
+    table = jnp.concatenate(
+        [position_ref[...].astype(jnp.float32), observed_ref[...]] + used, axis=0
+    )
+    out_ref[...] = jnp.broadcast_to(table[None], out_ref.shape)
+
+
+def table_of(count, position, observed, precision, patches):
+    vmem = pl.BlockSpec(memory_space=pltpu.VMEM)
+    return pl.pallas_call(
+        table_kernel,
+        in_specs=[pl.BlockSpec(memory_space=pltpu.SMEM)] + [vmem] * 3,
+        out_specs=vmem,
+        out_shape=jax.ShapeDtypeStruct((patches, 3 * OWN_BLOCKS, SLOTS), jnp.float32),
+    )(count, position, observed, precision)
 
 
 def turn_kernel(fields_ref, out_ref):
@@ -198,6 +217,45 @@
     )(fields)
 
 
+def gather_kernel(*refs):
+    by_depth, by_turn = refs[:DEPTHS], refs[DEPTHS:]
+    for turn in range(1, TURNS):
+        for depth in range(DEPTHS):
+            by_turn[turn - 1][depth] = by_depth[depth][turn]
+
+
+def gathered(by_depth):
+    turns, count, own, columns = by_depth[0].shape
+    return pl.pallas_call(
+        gather_kernel,
+        grid=(count // PAIR,),
+        in_specs=[pl.BlockSpec((turns, PAIR, own, columns), lambda v: (0, v, 0, 0))] * DEPTHS,
+        out_specs=[pl.BlockSpec((DEPTHS, PAIR, own, columns), lambda v: (0, v, 0, 0))] * (turns - 1),
+        out_shape=[
+            jax.ShapeDtypeStruct((DEPTHS, count, own, columns), by_depth[0].dtype)
+            for _ in range(turns - 1)
+        ],
+        compiler_params=PARAMS,
+        cost_estimate=pl.CostEstimate(flops=0, bytes_accessed=1 << 22, transcendentals=0),
+    )(*by_depth)
+
+
+def passed_kernel(cells_ref, out_ref):
+    out_ref[...] = cells_ref[...]
+
+
+def passed(cells):
+    vmem = pl.BlockSpec(memory_space=pltpu.VMEM)
+    return pl.pallas_call(
+        passed_kernel,
+        in_specs=[vmem],
+        out_specs=vmem,
+        out_shape=jax.ShapeDtypeStruct(cells.shape, cells.dtype),
+        compiler_params=PARAMS,
+        cost_estimate=pl.CostEstimate(flops=1 << 40, bytes_accessed=1 << 31, transcendentals=0),
+    )(cells)
+
+
 def analyse(weights, wide):
     mean = jnp.sum(wide, axis=0, keepdims=True) * (1.0 / wide.shape[0])
     pert = (wide - mean).astype(jnp.bfloat16)
@@ -205,31 +263,29 @@
 
 
 def apply_first_kernel(weights_ref, *refs):
-    by_depth, by_turn, out_refs = refs[:8], refs[8:11], refs[11:]
+    by_depth, by_turn, out_ref = refs[:DEPTHS], refs[DEPTHS:-1], refs[-1]
     own, columns = by_depth[0].shape[2:]
-    parts = [ref[0, 0].astype(jnp.float32) for ref in by_depth]
-    for ref in by_turn:
-        parts.append(ref[...].astype(jnp.float32).reshape(DEPTHS * own, columns))
-    updated = analyse(weights_ref[...], jnp.concatenate(parts, axis=0))
-    updated = updated.reshape(len(out_refs), TURNS * DEPTHS // len(out_refs), 1, own, columns)
-    for part, ref in enumerate(out_refs):
-        ref[...] = updated[part].astype(jnp.bfloat16)
-
-
-def apply_first(weights, by_depth, by_turn, parts, levels):
+    for level in range(PAIR):
+        parts = [ref[0, level].astype(jnp.float32) for ref in by_depth]
+        for ref in by_turn:
+            parts.append(ref[:, level].astype(jnp.float32).reshape(DEPTHS * own, columns))
+        updated = analyse(weights_ref[...], jnp.concatenate(parts, axis=0))
+        updated = updated.reshape(TURNS * DEPTHS, own, columns)
+        out_ref[:, level] = updated.astype(out_ref.dtype)
+
+
+def apply_first(weights, by_depth, by_turn, levels):
     _, count, own, columns = by_depth[0].shape
     members = weights.shape[0]
-    groups = TURNS * DEPTHS // parts
-    taken = pl.BlockSpec((DEPTHS, 1, own, columns), lambda v: (0, v, 0, 0))
-    given = pl.BlockSpec((groups, 1, own, columns), lambda v: (0, v, 0, 0))
+    groups = TURNS * DEPTHS
     return pl.pallas_call(
         apply_first_kernel,
-        grid=(count,),
+        grid=(count // PAIR,),
         in_specs=[pl.BlockSpec((members, members), lambda v: (0, 0))]
-        + [pl.BlockSpec((1, 1, own, columns), lambda v: (0, v, 0, 0))] * DEPTHS
-        + [taken] * (TURNS - 1),
-        out_specs=[given] * parts,
-        out_shape=[jax.ShapeDtypeStruct((groups, levels, own, columns), jnp.bfloat16)] * parts,
+        + [pl.BlockSpec((1, PAIR, own, columns), lambda v: (0, v, 0, 0))] * DEPTHS
+        + [pl.BlockSpec((DEPTHS, PAIR, own, columns), lambda v: (0, v, 0, 0))] * (TURNS - 1),
+        out_specs=pl.BlockSpec((groups, PAIR, own, columns), lambda v: (0, v, 0, 0)),
+        out_shape=jax.ShapeDtypeStruct((groups, levels, own, columns), jnp.bfloat16),
         compiler_params=PARAMS,
         cost_estimate=cost(members * count * columns, 2 * members * members * count * columns),
     )(weights, *by_depth, *by_turn)
@@ -293,18 +349,17 @@
     level = lax.axis_index("level")
     place = jnp.stack([here // DEPTHS, here % DEPTHS, level]).astype(jnp.int32)
 
-    slot_index = lax.broadcasted_iota(jnp.int32, precision.shape, 3)
-    precision_used = jnp.where(slot_index < valid_count[..., None], precision, 0.0)
-    table = jnp.concatenate(
-        [
-            position.reshape(OWN_BLOCKS, SLOTS).astype(jnp.float32),
+    tables = exchange(
+        table_of(
+            valid_count.reshape(OWN_BLOCKS),
+            position.reshape(OWN_BLOCKS, SLOTS),
             observations.reshape(OWN_BLOCKS, SLOTS),
-            precision_used.reshape(OWN_BLOCKS, SLOTS),
-        ]
-    )
-    tables = exchange(jnp.broadcast_to(table[None], (row_patches,) + table.shape))
-
-    packed = pack_first(place, turned_fields, 0, FIRST)
+            precision.reshape(OWN_BLOCKS, SLOTS),
+            row_patches,
+        )
+    )
+
+    packed = pack_first(place, turned_fields, FIRST)
     by_depth = [packed[0]] + [shifted(packed[depth], 0, depth) for depth in range(1, DEPTHS)]
 
     where = tables[:, :OWN_BLOCKS].reshape(row_patches, OWN_BLOCKS * SLOTS).astype(jnp.int32)
@@ -321,14 +376,12 @@
     near = exchange(spread).reshape(members, 3 * SLOTS)
 
     outgoing = turned(turned_fields, FIRST)
-    outgoing, near, by_depth[3], by_depth[5] = barrier(
-        (outgoing, near, by_depth[3], by_depth[5])
-    )
+    outgoing, near = barrier((outgoing, near))
+    near = passed(near)
+    near, by_depth[3], by_depth[5] = barrier((near, by_depth[3], by_depth[5]))
     incoming = exchange(outgoing)
-    by_turn = [
-        shifted(jnp.stack([piece[turn] for piece in by_depth]), turn, 0)
-        for turn in range(1, TURNS)
-    ]
+    by_turn = gathered(by_depth)
+    by_turn = [shifted(by_turn[turn - 1], turn, 0) for turn in range(1, TURNS)]
 
     pair_rows = jnp.pad(tables[:, OWN_BLOCKS:], ((1, 1), (0, 0), (0, 0)))
     pair_own = lax.dynamic_slice_in_dim(pair_rows, here, 3, axis=0)
@@ -342,7 +395,7 @@
         [swapped(cells) for cells in nears],
         [pair_above, pair_own, pair_below],
     )
-    outs = apply_first(sided, by_depth, by_turn, 1, VARIABLES)[0]
+    outs = apply_first(sided, by_depth, by_turn, VARIABLES)
     incoming, outs = barrier((incoming, outs))
     outs = apply_rest(weights, incoming, outs)
     whole = turned(exchange(outs), params=SMALL)

time: 347 us -> 330 us (0.951)
  waiting for transfers between devices: 76 us -> 67.4 us
  local copies, waits for them, and re-layouts: 7.46 us -> 2.14 us
    ppermute x10, waiting for transfers between devices: 29.5 us -> 18.9 us  [shifted(): return lax.ppermute(cells, 'member', pairs)]
    pallas_call x1 -> x4, Pallas kernels: 4.92 us -> 9.36 us  [the longest x1 3.67 us: apply_first(): pl.pallas_call(apply_first_kernel, grid=(count // PAIR,), in_specs=[pl.Bl...]
    unnamed x53 -> x40, local copies, waits for them, and re-layouts: 6.11 us -> 2.1 us
  transfers between devices with their start and end apart: 20 -> 20, of which waited for: 10 -> 10; matrix products, arithmetic and copies ran while one was open for 5% -> 4% of each run, Pallas kernels for 7% -> 8%
where the time goes in v3:
time: 330 us
  blocking collectives  149 us (45%)
  waiting for transfers between devices  67.4 us (20%)
  starting transfers between devices  61 us (18%)
  Pallas kernels  37.2 us (11%)
  matrix products  10.7 us (3%)
    all_to_all x1, blocking collectives, exchange(): lax.all_to_all(cells, 'member', split_axis=0, concat_axis=0, tiled=True)  145 us
    all_to_all x3, waiting for transfers between devices, exchange(): lax.all_to_all(cells, 'member', split_axis=0, concat_axis=0, tiled=True)  34.8 us
    all_to_all x3, starting transfers between devices, exchange(): lax.all_to_all(cells, 'member', split_axis=0, concat_axis=0, tiled=True)  28.1 us
    ppermute x10, starting transfers between devices, shifted(): return lax.ppermute(cells, 'member', pairs)  23.7 us
    ppermute x10, waiting for transfers between devices, shifted(): return lax.ppermute(cells, 'member', pairs)  18.9 us
    dot_general x1, matrix products, observe(): jnp.einsum('kpvq,pqo->kpvo', shaped_fields, column_hot, preferred_element...  10.7 us
    pallas_call x1, Pallas kernels, weights_for(): pl.pallas_call(weights_kernel, in_specs=[smem, smem] + [vmem] * 9, out_sp...  10.5 us
    ppermute x2, waiting for transfers between devices, row_halo(): above = lax.ppermute(cells, 'patch', [(i, i + 1) for i in range(count - 1)])  8.81 us
  transfers between devices with their start and end apart: 20, of which 10 were waited for; matrix products, arithmetic and copies ran while one was open for 4% of the time, Pallas kernels for 8%

profile of v3, /device:TPU:6, one launch (start us, length us, event | category | flops | bytes accessed | tf_op | source)
XLA Modules:
  0.0 329.5 jit_solution(16851588271023561624)
XLA Ops:
  1.5 11.5 %all-to-all-start = ((f32[32,6,128]{2,1,0:T(8,128)}), f32[32,6,128]{2,1,0:T(8,128)S(1)}, u32[]{:S(2)}, u32[]{:S(2)}) async-start(f32[32,6,128]{2,1,0:T(8,128)} %shard_map.74), calls=%async_computation | async-start | bytes 262144 | tf_op jit(solution)/shard_map/all_to_all | solution.py:25
  13.6 3.6 %shard_map.75 = (bf16[4,4,8,1024]{3,2,1,0:T(8,128)(2,1)}, bf16[4,4,8,1024]{3,2,1,0:T(8,128)(2,1)}, bf16[4,4,8,1024]{3,2,1,0:T(8,128)(2,1)}, bf16[4,4,8,1024]{3,2...) custom-call(s32[3]{0:T(128)} %pad_add_fusion.place_ref, ...), custom_call_target="tpu_custom_call" | custom-call | bytes 4194304 | tf_op jit(solution)/shard_map/pallas_call | solution.py:159
  22.0 2.7 collective-permute-start.3
  24.6 5.7 %collective-permute-start.4 = (bf16[4,4,8,1024]{3,2,1,0:T(8,128)(2,1)}, bf16[4,4,8,1024]{3,2,1,0:T(8,128)(2,1)S(1)}, u32[]{:S(2)}, u32[]{:S(2)}) collective-permute-start(bf16[4,4,8,1024]{3,2,1,0:T(8,128)(2,1)} %get-tuple-element.35), channel_id=1, source_target_pairs={{0,32},{8,40},{16,48},{24,56},{32,0},{40,8},{48,16},{56,24},{64,96... | collective-permute-start | bytes 786440 | tf_op jit(solution)/shard_map/ppermute | solution.py:40
  31.0 10.7 %fusion.5 = f32[8,32,256]{2,0,1:T(8,128)S(1)} fusion(bf16[8,32,12,1024]{3,1,2,0:T(8,128)(2,1)} %bitcast.59, s32[32,256]{1,0:T(8,128)S(1)} %get-tuple-element.60, f32[32,12,256]{2,1,0:T(8,128)S(1)} %fusion.10), kind=kOutput, calls=%fused_computation.6 | convolution fusion | flops 1620508672 | bytes 6979584 | tf_op jit(solution)/shard_map/kpvq,pqo->kpvo/dot_general | solution.py:331
  41.7 4.2 %all-reduce.3 = bf16[8,32,256]{2,0,1:T(8,128)(2,1)S(1)} all-reduce(f32[8,32,256]{2,0,1:T(8,128)S(1)} %fusion.5), channel_id=1, replica_groups=mesh['member'=32,'patch'=4,'level'=2] {'level'}, use_global_device_ids=true, to_apply=%region_1.2 | all-reduce | flops 65536 | bytes 393216 | tf_op jit(solution)/shard_map/psum | solution.py:367
  48.3 10.4 %all-to-all-start.1 = ((bf16[32,8,384]{2,1,0:T(8,128)(2,1)}), bf16[32,8,384]{2,1,0:T(8,128)(2,1)S(1)}, u32[]{:S(2)}, u32[]{:S(2)}) async-start(bf16[32,8,384]{2,1,0:T(8,128)(2,1)} %maximum_bitcast_fusion), calls=%async_computation.1 | async-start | bytes 393216 | tf_op jit(solution)/shard_map/all_to_all | solution.py:25
  58.7 3.7 %collective-permute-start.5 = (bf16[4,4,8,1024]{3,2,1,0:T(8,128)(2,1)}, bf16[4,4,8,1024]{3,2,1,0:T(8,128)(2,1)}, u32[]{:S(2)}, u32[]{:S(2)}) collective-permute-start(bf16[4,4,8,1024]{3,2,1,0:T(8,128)(2,1)} %get-tuple-element.38), channel_id=1, source_target_pairs={{0,24},{8,32},{16,40},{24,48},{32,56},{40,0},{48,8},{56,16},{64,88... | collective-permute-start | bytes 786440 | tf_op jit(solution)/shard_map/ppermute | solution.py:40
  63.9 4.1 %shard_map.73 = bf16[32,8,8,1024]{3,2,1,0:T(8,128)(2,1)} custom-call(bf16[8,12,32,1024]{3,2,1,0:T(8,128)(2,1)} %bitcast.60), custom_call_target="tpu_custom_call" | custom-call | bytes 12582912 | tf_op jit(solution)/shard_map/pallas_call | solution.py:209
  67.9 4.4 %all-to-all-done.1 = bf16[32,8,384]{2,1,0:T(8,128)(2,1)S(1)} async-done(((bf16[32,8,384]{2,1,0:T(8,128)(2,1)}), bf16[32,8,384]{2,1,0:T(8,128)(2,1)S(1)}, u32[]{:S(2)}, u32[]{:S(2)}) %all-to-all-start.1) | async-done | bytes 196640 | tf_op jit(solution)/shard_map/all_to_all | solution.py:25
  72.4 6.2 %all-to-all-start.2 = ((bf16[32,8,8,1024]{3,2,1,0:T(8,128)(2,1)}), bf16[32,8,8,1024]{3,2,1,0:T(8,128)(2,1)}, u32[]{:S(2)}, u32[]{:S(2)}) async-start(bf16[32,8,8,1024]{3,2,1,0:T(8,128)(2,1)} %shard_map.73), calls=%async_computation.2 | async-start | bytes 8388608 | tf_op jit(solution)/shard_map/all_to_all | solution.py:25
  80.2 6.4 %collective-permute-done.5.refs_3_ = bf16[4,4,8,1024]{3,2,1,0:T(8,128)(2,1)} collective-permute-done((bf16[4,4,8,1024]{3,2,1,0:T(8,128)(2,1)}, bf16[4,4,8,1024]{3,2,1,0:T(8,128)(2,1)}, u32[]{:S(2)}, u32[]{:S(2)}) %collective-permute-start.5) | collective-permute-done | bytes 262176 | tf_op jit(solution)/shard_map/ppermute | solution.py:40
  86.6 2.6 shard_map.78
  94.7 2.7 collective-permute-start.13
  100.0 4.5 %collective-permute-done.12.refs_6_ = f32[3,4,128]{2,1,0:T(4,128)S(1)} collective-permute-done((f32[3,4,128]{2,1,0:T(4,128)S(1)}, f32[3,4,128]{2,1,0:T(4,128)S(1)}, u32[]{:S(2)}, u32[]{:S(2)}) %collective-permute-start.12) | collective-permute-done | bytes 6176 | tf_op jit(solution)/shard_map/ppermute | solution.py:30
  104.5 3.9 %collective-permute-start.8 = (bf16[256,384]{1,0:T(8,128)(2,1)}, bf16[256,384]{1,0:T(8,128)(2,1)S(1)}, u32[]{:S(2)}, u32[]{:S(2)}) collective-permute-start(bf16[256,384]{1,0:T(8,128)(2,1)} %shard_map.76.refs_1_), channel_id=1, source_target_pairs={{2,0},{4,2},{6,4},{3,1},{5,3},{7,5},{10,8},{12,10},{14,12},{11,9},... | collective-permute-start | bytes 589832 | tf_op jit(solution)/shard_map/ppermute | solution.py:31
  111.9 4.3 %collective-permute-done.7.refs_0_ = bf16[256,384]{1,0:T(8,128)(2,1)S(1)} collective-permute-done((bf16[256,384]{1,0:T(8,128)(2,1)}, bf16[256,384]{1,0:T(8,128)(2,1)S(1)}, u32[]{:S(2)}, u32[]{:S(2)}) %collective-permute-start.7) | collective-permute-done | bytes 196640 | tf_op jit(solution)/shard_map/ppermute | solution.py:30
  118.4 10.5 %shard_map.77 = (bf16[256,256]{1,0:T(8,128)(2,1)}, bf16[256,256]{1,0:T(8,128)(2,1)}) custom-call(s32[8]{0:T(128)} %bitcast.68, s32[3]{0:T(128)} %pad_add_fusion.place_ref, bf16[256,384]{1,0:T(8,128)(2,1)} %copy-done.13, bf16[256,384]{1,0:T(8,128)(2,1)} %shard_map.76.refs_1_, bf16[256,384]{1,0:T(8,128)(2,1)} %copy-done.12, bf16[256,384]{1,0:T(8,128)(2,1)} %copy-done.15, ...), custom_call_target="tpu_custom_call" | custom-call | bytes 1024 | tf_op jit(solution)/shard_map/pallas_call | solution.py:131
  128.9 10.9 %collective-permute-done.15.refs_9_ = bf16[8,4,8,1024]{3,2,1,0:T(8,128)(2,1)S(1)} collective-permute-done((bf16[8,4,8,1024]{3,2,1,0:T(8,128)(2,1)}, bf16[8,4,8,1024]{3,2,1,0:T(8,128)(2,1)S(1)}, u32[]{:S(2)}, u32[]{:S(2)}) %collective-permute-start.15) | collective-permute-done | bytes 524320 | tf_op jit(solution)/shard_map/ppermute | solution.py:40
  140.7 3.7 %shard_map.79._ = bf16[32,12,8,1024]{3,2,1,0:T(8,128)(2,1)} custom-call(bf16[256,256]{1,0:T(8,128)(2,1)} %get-tuple-element.43.weights_ref, bf16[4,4,8,1024]{3,2,1,0:T(8,128)(2,1)} %get-tuple-element.44.refs_0_, bf16[4,4,8,1024]{3,2,1,0:T(8,128)(2,1)} %copy-done, bf16[4,4,8,1024]{3,2,1,0:T(8,128)(2,1)} %copy-done.2, ...), custom_call_target="tpu_custom_call" | custom-call | flops 536870912 | bytes 4194304 | tf_op jit(solution)/shard_map/pallas_call | solution.py:281
  144.4 30.4 %all-to-all-done.2.fields_ref = bf16[32,8,8,1024]{3,2,1,0:T(8,128)(2,1)} async-done(((bf16[32,8,8,1024]{3,2,1,0:T(8,128)(2,1)}), bf16[32,8,8,1024]{3,2,1,0:T(8,128)(2,1)}, u32[]{:S(2)}, u32[]{:S(2)}) %all-to-all-start.2) | async-done | bytes 4194336 | tf_op jit(solution)/shard_map/all_to_all | solution.py:25
  174.7 5.6 %shard_map.80 = bf16[32,12,8,1024]{3,2,1,0:T(8,128)(2,1)} custom-call(bf16[256,256]{1,0:T(8,128)(2,1)} %get-tuple-element.41.weights_ref, bf16[32,8,8,1024]{3,2,1,0:T(8,128)(2,1)} %all-to-all-done.2.fields_ref, bf16[32,12,8,1024]{3,2,1,0:T(8,128)(2,1)} %shard_map.79._), custom_call_target="tpu_custom_call", output_to_operand_aliasing={{}: (2, {})} | custom-call | flops 1073741824 | bytes 8388608 | tf_op jit(solution)/shard_map/pallas_call | solution.py:306
  180.3 145.2 %all_to_all.20.fields_ref = bf16[32,12,8,1024]{3,2,1,0:T(8,128)(2,1)S(1)} all-to-all(bf16[32,12,8,1024]{3,2,1,0:T(8,128)(2,1)} %shard_map.80), channel_id=1, replica_groups=mesh['member'=32,'patch'=4,'level'=2] {'member'}, dimensions={0} | all-to-all | bytes 12582912 | tf_op jit(solution)/shard_map/all_to_all | solution.py:25
  325.5 4.0 %shard_map.81 = bf16[8,12,32,1024]{3,2,1,0:T(8,128)(2,1)} custom-call(bf16[32,12,8,1024]{3,2,1,0:T(8,128)(2,1)S(1)} %all_to_all.20.fields_ref), custom_call_target="tpu_custom_call" | custom-call | bytes 12582912 | tf_op jit(solution)/shard_map/pallas_call | solution.py:209
  (77 shorter events, 27.6 us)
Async XLA Ops:
  0.0 30.4 %copy-start.19 = (f32[1,12]{1,0:T(1,128)S(1)}, f32[1,12]{1,0:T(1,128)}, u32[]{:S(2)}) copy-start(f32[1,12]{1,0:T(1,128)} %param.12) | copy-start | bytes 148
  1.5 28.9 %all-to-all-start = ((f32[32,6,128]{2,1,0:T(8,128)}), f32[32,6,128]{2,1,0:T(8,128)S(1)}, u32[]{:S(2)}, u32[]{:S(2)}) async-start(f32[32,6,128]{2,1,0:T(8,128)} %shard_map.74), calls=%async_computation | async-start | bytes 262144 | tf_op jit(solution)/shard_map/all_to_all | solution.py:25
  17.2 29.4 %collective-permute-start = (bf16[4,4,8,1024]{3,2,1,0:T(8,128)(2,1)}, bf16[4,4,8,1024]{3,2,1,0:T(8,128)(2,1)S(1)}, u32[]{:S(2)}, u32[]{:S(2)}) collective-permute-start(bf16[4,4,8,1024]{3,2,1,0:T(8,128)(2,1)} %get-tuple-element.31), channel_id=1, source_target_pairs={{0,8},{8,16},{16,24},{24,32},{32,40},{40,48},{48,56},{56,0},{64,72... | collective-permute-start | bytes 786440 | tf_op jit(solution)/shard_map/ppermute | solution.py:40
  19.0 27.6 %collective-permute-start.1 = (bf16[4,4,8,1024]{3,2,1,0:T(8,128)(2,1)}, bf16[4,4,8,1024]{3,2,1,0:T(8,128)(2,1)S(1)}, u32[]{:S(2)}, u32[]{:S(2)}) collective-permute-start(bf16[4,4,8,1024]{3,2,1,0:T(8,128)(2,1)} %get-tuple-element.32), channel_id=1, source_target_pairs={{0,56},{8,0},{16,8},{24,16},{32,24},{40,32},{48,40},{56,48},{64,12... | collective-permute-start | bytes 786440 | tf_op jit(solution)/shard_map/ppermute | solution.py:40
  20.5 26.1 %collective-permute-start.2 = (bf16[4,4,8,1024]{3,2,1,0:T(8,128)(2,1)}, bf16[4,4,8,1024]{3,2,1,0:T(8,128)(2,1)S(1)}, u32[]{:S(2)}, u32[]{:S(2)}) collective-permute-start(bf16[4,4,8,1024]{3,2,1,0:T(8,128)(2,1)} %get-tuple-element.33), channel_id=1, source_target_pairs={{0,16},{8,24},{16,32},{24,40},{32,48},{40,56},{48,0},{56,8},{64,80... | collective-permute-start | bytes 786440 | tf_op jit(solution)/shard_map/ppermute | solution.py:40
  22.0 26.3 %collective-permute-start.3 = (bf16[4,4,8,1024]{3,2,1,0:T(8,128)(2,1)}, bf16[4,4,8,1024]{3,2,1,0:T(8,128)(2,1)S(1)}, u32[]{:S(2)}, u32[]{:S(2)}) collective-permute-start(bf16[4,4,8,1024]{3,2,1,0:T(8,128)(2,1)} %get-tuple-element.34), channel_id=1, source_target_pairs={{0,48},{8,56},{16,0},{24,8},{32,16},{40,24},{48,32},{56,40},{64,11... | collective-permute-start | bytes 786440 | tf_op jit(solution)/shard_map/ppermute | solution.py:40
  24.6 23.7 %collective-permute-start.4 = (bf16[4,4,8,1024]{3,2,1,0:T(8,128)(2,1)}, bf16[4,4,8,1024]{3,2,1,0:T(8,128)(2,1)S(1)}, u32[]{:S(2)}, u32[]{:S(2)}) collective-permute-start(bf16[4,4,8,1024]{3,2,1,0:T(8,128)(2,1)} %get-tuple-element.35), channel_id=1, source_target_pairs={{0,32},{8,40},{16,48},{24,56},{32,0},{40,8},{48,16},{56,24},{64,96... | collective-permute-start | bytes 786440 | tf_op jit(solution)/shard_map/ppermute | solution.py:40
  46.6 25.8 %copy-start = (bf16[4,4,8,1024]{3,2,1,0:T(8,128)(2,1)}, bf16[4,4,8,1024]{3,2,1,0:T(8,128)(2,1)S(1)}, u32[]{:S(2)}) copy-start(bf16[4,4,8,1024]{3,2,1,0:T(8,128)(2,1)S(1)} %collective-permute-done.refs_1_) | copy-start | bytes 786436
  46.6 25.8 %copy-start.1 = (bf16[4,4,8,1024]{3,2,1,0:T(8,128)(2,1)}, bf16[4,4,8,1024]{3,2,1,0:T(8,128)(2,1)S(1)}, u32[]{:S(2)}) copy-start(bf16[4,4,8,1024]{3,2,1,0:T(8,128)(2,1)S(1)} %collective-permute-done.1.refs_7_) | copy-start | bytes 786436
  46.6 25.7 %copy-start.2 = (bf16[4,4,8,1024]{3,2,1,0:T(8,128)(2,1)}, bf16[4,4,8,1024]{3,2,1,0:T(8,128)(2,1)S(1)}, u32[]{:S(2)}) copy-start(bf16[4,4,8,1024]{3,2,1,0:T(8,128)(2,1)S(1)} %collective-permute-done.2.refs_2_) | copy-start | bytes 786436
  48.3 24.0 %all-to-all-start.1 = ((bf16[32,8,384]{2,1,0:T(8,128)(2,1)}), bf16[32,8,384]{2,1,0:T(8,128)(2,1)S(1)}, u32[]{:S(2)}, u32[]{:S(2)}) async-start(bf16[32,8,384]{2,1,0:T(8,128)(2,1)} %maximum_bitcast_fusion), calls=%async_computation.1 | async-start | bytes 393216 | tf_op jit(solution)/shard_map/all_to_all | solution.py:25
  58.7 27.9 %collective-permute-start.5 = (bf16[4,4,8,1024]{3,2,1,0:T(8,128)(2,1)}, bf16[4,4,8,1024]{3,2,1,0:T(8,128)(2,1)}, u32[]{:S(2)}, u32[]{:S(2)}) collective-permute-start(bf16[4,4,8,1024]{3,2,1,0:T(8,128)(2,1)} %get-tuple-element.38), channel_id=1, source_target_pairs={{0,24},{8,32},{16,40},{24,48},{32,56},{40,0},{48,8},{56,16},{64,88... | collective-permute-start | bytes 786440 | tf_op jit(solution)/shard_map/ppermute | solution.py:40
  62.4 24.2 %collective-permute-start.6 = (bf16[4,4,8,1024]{3,2,1,0:T(8,128)(2,1)}, bf16[4,4,8,1024]{3,2,1,0:T(8,128)(2,1)}, u32[]{:S(2)}, u32[]{:S(2)}) collective-permute-start(bf16[4,4,8,1024]{3,2,1,0:T(8,128)(2,1)} %get-tuple-element.39), channel_id=1, source_target_pairs={{0,40},{8,48},{16,56},{24,0},{32,8},{40,16},{48,24},{56,32},{64,10... | collective-permute-start | bytes 786440 | tf_op jit(solution)/shard_map/ppermute | solution.py:40
  72.4 102.4 %all-to-all-start.2 = ((bf16[32,8,8,1024]{3,2,1,0:T(8,128)(2,1)}), bf16[32,8,8,1024]{3,2,1,0:T(8,128)(2,1)}, u32[]{:S(2)}, u32[]{:S(2)}) async-start(bf16[32,8,8,1024]{3,2,1,0:T(8,128)(2,1)} %shard_map.73), calls=%async_computation.2 | async-start | bytes 8388608 | tf_op jit(solution)/shard_map/all_to_all | solution.py:25
  86.6 21.8 %collective-permute-start.10 = (bf16[256,384]{1,0:T(8,128)(2,1)}, bf16[256,384]{1,0:T(8,128)(2,1)S(1)}, u32[]{:S(2)}, u32[]{:S(2)}) collective-permute-start(bf16[256,384]{1,0:T(8,128)(2,1)} %shard_map.76.refs_1_), channel_id=1, source_target_pairs={{0,1},{1,0},{2,3},{3,2},{4,5},{5,4},{6,7},{7,6},{8,9},{9,8},{10,11... | collective-permute-start | bytes 589832 | tf_op jit(solution)/shard_map/ppermute | solution.py:44
  89.2 39.7 %collective-permute-start.14 = (bf16[8,4,8,1024]{3,2,1,0:T(8,128)(2,1)}, bf16[8,4,8,1024]{3,2,1,0:T(8,128)(2,1)S(1)}, u32[]{:S(2)}, u32[]{:S(2)}) collective-permute-start(bf16[8,4,8,1024]{3,2,1,0:T(8,128)(2,1)} %get-tuple-element.52), channel_id=1, source_target_pairs={{0,64},{8,72},{16,80},{24,88},{32,96},{40,104},{48,112},{56,120},{... | collective-permute-start | bytes 1572872 | tf_op jit(solution)/shard_map/ppermute | solution.py:40
  90.5 49.2 %collective-permute-start.15 = (bf16[8,4,8,1024]{3,2,1,0:T(8,128)(2,1)}, bf16[8,4,8,1024]{3,2,1,0:T(8,128)(2,1)S(1)}, u32[]{:S(2)}, u32[]{:S(2)}) collective-permute-start(bf16[8,4,8,1024]{3,2,1,0:T(8,128)(2,1)} %get-tuple-element.53), channel_id=1, source_target_pairs={{0,128},{8,136},{16,144},{24,152},{32,160},{40,168},{48,176},{56,1... | collective-permute-start | bytes 1572872 | tf_op jit(solution)/shard_map/ppermute | solution.py:40
  92.9 46.8 %collective-permute-start.16 = (bf16[8,4,8,1024]{3,2,1,0:T(8,128)(2,1)}, bf16[8,4,8,1024]{3,2,1,0:T(8,128)(2,1)S(1)}, u32[]{:S(2)}, u32[]{:S(2)}) collective-permute-start(bf16[8,4,8,1024]{3,2,1,0:T(8,128)(2,1)} %get-tuple-element.54), channel_id=1, source_target_pairs={{0,192},{8,200},{16,208},{24,216},{32,224},{40,232},{48,240},{56,2... | collective-permute-start | bytes 1572872 | tf_op jit(solution)/shard_map/ppermute | solution.py:40
  94.7 4.1 %collective-permute-start.13 = (f32[3,4,128]{2,1,0:T(4,128)S(1)}, f32[3,4,128]{2,1,0:T(4,128)S(1)}, u32[]{:S(2)}, u32[]{:S(2)}) collective-permute-start(f32[3,4,128]{2,1,0:T(4,128)S(1)} %pad_dynamic-slice_fusion.refs_7_), channel_id=1, source_target_pairs={{2,0},{4,2},{6,4},{3,1},{5,3},{7,5},{10,8},{12,10},{14,12},{11,9},... | collective-permute-start | bytes 18440 | tf_op jit(solution)/shard_map/ppermute | solution.py:31
  98.7 5.8 %collective-permute-start.12 = (f32[3,4,128]{2,1,0:T(4,128)S(1)}, f32[3,4,128]{2,1,0:T(4,128)S(1)}, u32[]{:S(2)}, u32[]{:S(2)}) collective-permute-start(f32[3,4,128]{2,1,0:T(4,128)S(1)} %pad_dynamic-slice_fusion.refs_7_), channel_id=1, source_target_pairs={{0,2},{2,4},{4,6},{1,3},{3,5},{5,7},{8,10},{10,12},{12,14},{9,11},... | collective-permute-start | bytes 18440 | tf_op jit(solution)/shard_map/ppermute | solution.py:30
  104.5 7.4 %collective-permute-start.8 = (bf16[256,384]{1,0:T(8,128)(2,1)}, bf16[256,384]{1,0:T(8,128)(2,1)S(1)}, u32[]{:S(2)}, u32[]{:S(2)}) collective-permute-start(bf16[256,384]{1,0:T(8,128)(2,1)} %shard_map.76.refs_1_), channel_id=1, source_target_pairs={{2,0},{4,2},{6,4},{3,1},{5,3},{7,5},{10,8},{12,10},{14,12},{11,9},... | collective-permute-start | bytes 589832 | tf_op jit(solution)/shard_map/ppermute | solution.py:31
  108.5 7.8 %collective-permute-start.7 = (bf16[256,384]{1,0:T(8,128)(2,1)}, bf16[256,384]{1,0:T(8,128)(2,1)S(1)}, u32[]{:S(2)}, u32[]{:S(2)}) collective-permute-start(bf16[256,384]{1,0:T(8,128)(2,1)} %shard_map.76.refs_1_), channel_id=1, source_target_pairs={{0,2},{2,4},{4,6},{1,3},{3,5},{5,7},{8,10},{10,12},{12,14},{9,11},... | collective-permute-start | bytes 589832 | tf_op jit(solution)/shard_map/ppermute | solution.py:30
  111.9 4.3 %collective-permute-start.11 = (bf16[256,384]{1,0:T(8,128)(2,1)S(1)}, bf16[256,384]{1,0:T(8,128)(2,1)S(1)}, u32[]{:S(2)}, u32[]{:S(2)}) collective-permute-start(bf16[256,384]{1,0:T(8,128)(2,1)S(1)} %collective-permute-done.8.refs_2_), channel_id=1, source_target_pairs={{0,1},{1,0},{2,3},{3,2},{4,5},{5,4},{6,7},{7,6},{8,9},{9,8},{10,11... | collective-permute-start | bytes 589832 | tf_op jit(solution)/shard_map/ppermute | solution.py:44
  116.3 1.4 collective-permute-start.9
  (16 other events, 157.5 us)

commit v4 on v3

--- a/solution.py
+++ b/solution.py
@@ -11,8 +11,8 @@
 OWN_BLOCKS = 2
 LISTED = 8
 SWEEPS = 6
-FIRST = 4
-STEP = 4
+FIRST = 6
+STEP = 3
 PAIR = 2
 DEPTHS = 8
 TURNS = 4
@@ -370,13 +370,13 @@
     spread = jnp.concatenate(
         [padded[:, shift : shift + row_patches] for shift in range(3)], axis=2
     ).transpose(1, 0, 2)
-    spread, by_depth[1], by_depth[7], by_depth[2], by_depth[6], by_depth[4] = barrier(
-        (spread, by_depth[1], by_depth[7], by_depth[2], by_depth[6], by_depth[4])
-    )
+    spread, by_depth[1], by_depth[7] = barrier((spread, by_depth[1], by_depth[7]))
     near = exchange(spread).reshape(members, 3 * SLOTS)
 
     outgoing = turned(turned_fields, FIRST)
-    outgoing, near = barrier((outgoing, near))
+    outgoing, near, by_depth[2], by_depth[4], by_depth[6] = barrier(
+        (outgoing, near, by_depth[2], by_depth[4], by_depth[6])
+    )
     near = passed(near)
     near, by_depth[3], by_depth[5] = barrier((near, by_depth[3], by_depth[5]))
     incoming = exchange(outgoing)

time: 330 us -> 328 us (level)
  waiting for transfers between devices: 67.4 us -> 54.4 us
  blocking collectives: 149 us -> 157 us
  Pallas kernels: 37.2 us -> 40.6 us
    all_to_all x3, waiting for transfers between devices: 34.8 us -> 6.91 us  [exchange(): lax.all_to_all(cells, 'member', split_axis=0, concat_axis=0, tiled=True)]
    ppermute x10, waiting for transfers between devices: 18.9 us -> 33.7 us  [shifted(): return lax.ppermute(cells, 'member', pairs)]
    all_to_all x1, blocking collectives: 145 us -> 153 us  [exchange(): lax.all_to_all(cells, 'member', split_axis=0, concat_axis=0, tiled=True)]
  transfers between devices with their start and end apart: 20 -> 20, of which waited for: 10 -> 11; matrix products, arithmetic and copies ran while one was open for 4% -> 4% of each run, Pallas kernels for 8% -> 9%
where the time goes in v4:
time: 328 us; the launch traced here: 327 us
  blocking collectives  157 us (48%)
  starting transfers between devices  60.3 us (18%)
  waiting for transfers between devices  54.4 us (17%)
  Pallas kernels  40.6 us (12%)
  matrix products  10.7 us (3%)
    all_to_all x1, blocking collectives, exchange(): lax.all_to_all(cells, 'member', split_axis=0, concat_axis=0, tiled=True)  153 us
    ppermute x10, waiting for transfers between devices, shifted(): return lax.ppermute(cells, 'member', pairs)  33.7 us
    all_to_all x3, starting transfers between devices, exchange(): lax.all_to_all(cells, 'member', split_axis=0, concat_axis=0, tiled=True)  27.2 us
    ppermute x10, starting transfers between devices, shifted(): return lax.ppermute(cells, 'member', pairs)  23.9 us
    dot_general x1, matrix products, observe(): jnp.einsum('kpvq,pqo->kpvo', shaped_fields, column_hot, preferred_element...  10.7 us
    pallas_call x1, Pallas kernels, weights_for(): pl.pallas_call(weights_kernel, in_specs=[smem, smem] + [vmem] * 9, out_sp...  10.5 us
    ppermute x2, waiting for transfers between devices, row_halo(): above = lax.ppermute(cells, 'patch', [(i, i + 1) for i in range(count - 1)])  8.77 us
    pallas_call x2, Pallas kernels, turned(): pl.pallas_call(turn_kernel, grid=(levels // STEP,), in_specs=[pl.BlockSpe...  7.36 us
  transfers between devices with their start and end apart: 20, of which 11 were waited for; matrix products, arithmetic and copies ran while one was open for 4% of the time, Pallas kernels for 9%

profile of v4, /device:TPU:6, one launch (start us, length us, event | category | flops | bytes accessed | tf_op | source)
XLA Modules:
  0.0 327.3 jit_solution(7881180019685506205)
XLA Ops:
  1.5 11.5 %all-to-all-start = ((f32[32,6,128]{2,1,0:T(8,128)}), f32[32,6,128]{2,1,0:T(8,128)S(1)}, u32[]{:S(2)}, u32[]{:S(2)}) async-start(f32[32,6,128]{2,1,0:T(8,128)} %shard_map.74), calls=%async_computation | async-start | bytes 262144 | tf_op jit(solution)/shard_map/all_to_all | solution.py:25
  13.6 5.6 %shard_map.75 = (bf16[4,6,8,1024]{3,2,1,0:T(8,128)(2,1)}, bf16[4,6,8,1024]{3,2,1,0:T(8,128)(2,1)}, bf16[4,6,8,1024]{3,2,1,0:T(8,128)(2,1)}, bf16[4,6,8,1024]{3,2...) custom-call(s32[3]{0:T(128)} %pad_add_fusion.place_ref, ...), custom_call_target="tpu_custom_call" | custom-call | bytes 6291456 | tf_op jit(solution)/shard_map/pallas_call | solution.py:159
  23.9 4.2 %collective-permute-start.3 = (bf16[4,6,8,1024]{3,2,1,0:T(8,128)(2,1)}, bf16[4,6,8,1024]{3,2,1,0:T(8,128)(2,1)S(1)}, u32[]{:S(2)}, u32[]{:S(2)}) collective-permute-start(bf16[4,6,8,1024]{3,2,1,0:T(8,128)(2,1)} %get-tuple-element.35), channel_id=1, source_target_pairs={{0,32},{8,40},{16,48},{24,56},{32,0},{40,8},{48,16},{56,24},{64,96... | collective-permute-start | bytes 1179656 | tf_op jit(solution)/shard_map/ppermute | solution.py:40
  28.2 4.1 %collective-permute-start.4 = (bf16[4,6,8,1024]{3,2,1,0:T(8,128)(2,1)}, bf16[4,6,8,1024]{3,2,1,0:T(8,128)(2,1)S(1)}, u32[]{:S(2)}, u32[]{:S(2)}) collective-permute-start(bf16[4,6,8,1024]{3,2,1,0:T(8,128)(2,1)} %get-tuple-element.36), channel_id=1, source_target_pairs={{0,48},{8,56},{16,0},{24,8},{32,16},{40,24},{48,32},{56,40},{64,11... | collective-permute-start | bytes 1179656 | tf_op jit(solution)/shard_map/ppermute | solution.py:40
  32.9 10.7 %fusion.5 = f32[8,32,256]{2,0,1:T(8,128)S(1)} fusion(bf16[8,32,12,1024]{3,1,2,0:T(8,128)(2,1)} %bitcast.59, s32[32,256]{1,0:T(8,128)S(1)} %get-tuple-element.60, f32[32,12,256]{2,1,0:T(8,128)S(1)} %fusion.10), kind=kOutput, calls=%fused_computation.6 | convolution fusion | flops 1620508672 | bytes 6979584 | tf_op jit(solution)/shard_map/kpvq,pqo->kpvo/dot_general | solution.py:331
  43.6 4.2 %all-reduce.3 = bf16[8,32,256]{2,0,1:T(8,128)(2,1)S(1)} all-reduce(f32[8,32,256]{2,0,1:T(8,128)S(1)} %fusion.5), channel_id=1, replica_groups=mesh['member'=32,'patch'=4,'level'=2] {'level'}, use_global_device_ids=true, to_apply=%region_1.2 | all-reduce | flops 65536 | bytes 393216 | tf_op jit(solution)/shard_map/psum | solution.py:367
  48.6 6.2 %all-to-all-start.1 = ((bf16[32,8,384]{2,1,0:T(8,128)(2,1)}), bf16[32,8,384]{2,1,0:T(8,128)(2,1)S(1)}, u32[]{:S(2)}, u32[]{:S(2)}) async-start(bf16[32,8,384]{2,1,0:T(8,128)(2,1)} %maximum_bitcast_fusion), calls=%async_computation.1 | async-start | bytes 393216 | tf_op jit(solution)/shard_map/all_to_all | solution.py:25
  54.8 3.7 %collective-permute-start.5 = (bf16[4,6,8,1024]{3,2,1,0:T(8,128)(2,1)}, bf16[4,6,8,1024]{3,2,1,0:T(8,128)(2,1)}, u32[]{:S(2)}, u32[]{:S(2)}) collective-permute-start(bf16[4,6,8,1024]{3,2,1,0:T(8,128)(2,1)} %get-tuple-element.38), channel_id=1, source_target_pairs={{0,24},{8,32},{16,40},{24,48},{32,56},{40,0},{48,8},{56,16},{64,88... | collective-permute-start | bytes 1179656 | tf_op jit(solution)/shard_map/ppermute | solution.py:40
  59.9 3.4 %shard_map.73 = bf16[32,6,8,1024]{3,2,1,0:T(8,128)(2,1)} custom-call(bf16[8,12,32,1024]{3,2,1,0:T(8,128)(2,1)} %bitcast.60), custom_call_target="tpu_custom_call" | custom-call | bytes 12582912 | tf_op jit(solution)/shard_map/pallas_call | solution.py:209
  63.4 7.5 %collective-permute-done.4.refs_6_ = bf16[4,6,8,1024]{3,2,1,0:T(8,128)(2,1)S(1)} collective-permute-done((bf16[4,6,8,1024]{3,2,1,0:T(8,128)(2,1)}, bf16[4,6,8,1024]{3,2,1,0:T(8,128)(2,1)S(1)}, u32[]{:S(2)}, u32[]{:S(2)}) %collective-permute-start.4) | collective-permute-done | bytes 393248 | tf_op jit(solution)/shard_map/ppermute | solution.py:40
  70.9 6.9 %all-to-all-done.1 = bf16[32,8,384]{2,1,0:T(8,128)(2,1)S(1)} async-done(((bf16[32,8,384]{2,1,0:T(8,128)(2,1)}), bf16[32,8,384]{2,1,0:T(8,128)(2,1)S(1)}, u32[]{:S(2)}, u32[]{:S(2)}) %all-to-all-start.1) | async-done | bytes 196640 | tf_op jit(solution)/shard_map/all_to_all | solution.py:25
  77.8 9.5 %all-to-all-start.2 = ((bf16[32,6,8,1024]{3,2,1,0:T(8,128)(2,1)}), bf16[32,6,8,1024]{3,2,1,0:T(8,128)(2,1)}, u32[]{:S(2)}, u32[]{:S(2)}) async-start(bf16[32,6,8,1024]{3,2,1,0:T(8,128)(2,1)} %shard_map.73), calls=%async_computation.2 | async-start | bytes 6291456 | tf_op jit(solution)/shard_map/all_to_all | solution.py:25
  89.0 9.6 %collective-permute-done.5.refs_3_ = bf16[4,6,8,1024]{3,2,1,0:T(8,128)(2,1)} collective-permute-done((bf16[4,6,8,1024]{3,2,1,0:T(8,128)(2,1)}, bf16[4,6,8,1024]{3,2,1,0:T(8,128)(2,1)}, u32[]{:S(2)}, u32[]{:S(2)}) %collective-permute-start.5) | collective-permute-done | bytes 393248 | tf_op jit(solution)/shard_map/ppermute | solution.py:40
  99.0 4.1 %shard_map.78 = (bf16[8,6,8,1024]{3,2,1,0:T(8,128)(2,1)}, bf16[8,6,8,1024]{3,2,1,0:T(8,128)(2,1)}, bf16[8,6,8,1024]{3,2,1,0:T(8,128)(2,1)}) custom-call(bf16[4,6,8,1024]{3,2,1,0:T(8,128)(2,1)} %get-tuple-element.44.refs_0_, bf16[4,6,8,1024]{3,2,1,0:T(8,128)(2,1)} %copy-done, bf16[4,6,8,1024]{3,2,1,0:T(8,128)(2,1)} %copy-done.2, ...), custom_call_target="tpu_custom_call" | custom-call | bytes 4194304 | tf_op jit(solution)/shard_map/pallas_call | solution.py:229
  108.8 2.7 collective-permute-start.13
  114.2 4.5 %collective-permute-done.12.refs_6_ = f32[3,4,128]{2,1,0:T(4,128)S(1)} collective-permute-done((f32[3,4,128]{2,1,0:T(4,128)S(1)}, f32[3,4,128]{2,1,0:T(4,128)S(1)}, u32[]{:S(2)}, u32[]{:S(2)}) %collective-permute-start.12) | collective-permute-done | bytes 6176 | tf_op jit(solution)/shard_map/ppermute | solution.py:30
  118.7 3.9 %collective-permute-start.8 = (bf16[256,384]{1,0:T(8,128)(2,1)}, bf16[256,384]{1,0:T(8,128)(2,1)S(1)}, u32[]{:S(2)}, u32[]{:S(2)}) collective-permute-start(bf16[256,384]{1,0:T(8,128)(2,1)} %shard_map.76.refs_1_), channel_id=1, source_target_pairs={{2,0},{4,2},{6,4},{3,1},{5,3},{7,5},{10,8},{12,10},{14,12},{11,9},... | collective-permute-start | bytes 589832 | tf_op jit(solution)/shard_map/ppermute | solution.py:31
  126.1 4.3 %collective-permute-done.7.refs_0_ = bf16[256,384]{1,0:T(8,128)(2,1)S(1)} collective-permute-done((bf16[256,384]{1,0:T(8,128)(2,1)}, bf16[256,384]{1,0:T(8,128)(2,1)S(1)}, u32[]{:S(2)}, u32[]{:S(2)}) %collective-permute-start.7) | collective-permute-done | bytes 196640 | tf_op jit(solution)/shard_map/ppermute | solution.py:30
  132.5 10.5 %shard_map.77 = (bf16[256,256]{1,0:T(8,128)(2,1)}, bf16[256,256]{1,0:T(8,128)(2,1)}) custom-call(s32[8]{0:T(128)} %bitcast.68, s32[3]{0:T(128)} %pad_add_fusion.place_ref, bf16[256,384]{1,0:T(8,128)(2,1)} %copy-done.13, bf16[256,384]{1,0:T(8,128)(2,1)} %shard_map.76.refs_1_, bf16[256,384]{1,0:T(8,128)(2,1)} %copy-done.12, bf16[256,384]{1,0:T(8,128)(2,1)} %copy-done.15, ...), custom_call_target="tpu_custom_call" | custom-call | bytes 1024 | tf_op jit(solution)/shard_map/pallas_call | solution.py:131
  143.0 15.9 %collective-permute-done.15.refs_9_ = bf16[8,6,8,1024]{3,2,1,0:T(8,128)(2,1)S(1)} collective-permute-done((bf16[8,6,8,1024]{3,2,1,0:T(8,128)(2,1)}, bf16[8,6,8,1024]{3,2,1,0:T(8,128)(2,1)S(1)}, u32[]{:S(2)}, u32[]{:S(2)}) %collective-permute-start.15) | collective-permute-done | bytes 786464 | tf_op jit(solution)/shard_map/ppermute | solution.py:40
  160.1 5.3 %shard_map.79._ = bf16[32,12,8,1024]{3,2,1,0:T(8,128)(2,1)} custom-call(bf16[256,256]{1,0:T(8,128)(2,1)} %get-tuple-element.43.weights_ref, bf16[4,6,8,1024]{3,2,1,0:T(8,128)(2,1)} %get-tuple-element.44.refs_0_, bf16[4,6,8,1024]{3,2,1,0:T(8,128)(2,1)} %copy-done, bf16[4,6,8,1024]{3,2,1,0:T(8,128)(2,1)} %copy-done.2, ...), custom_call_target="tpu_custom_call" | custom-call | flops 805306368 | bytes 6291456 | tf_op jit(solution)/shard_map/pallas_call | solution.py:281
  165.4 4.6 %shard_map.80 = bf16[32,12,8,1024]{3,2,1,0:T(8,128)(2,1)} custom-call(bf16[256,256]{1,0:T(8,128)(2,1)} %get-tuple-element.41.weights_ref, bf16[32,6,8,1024]{3,2,1,0:T(8,128)(2,1)} %all-to-all-done.2.fields_ref, bf16[32,12,8,1024]{3,2,1,0:T(8,128)(2,1)} %shard_map.79._), custom_call_target="tpu_custom_call", output_to_operand_aliasing={{}: (2, {})} | custom-call | flops 805306368 | bytes 6291456 | tf_op jit(solution)/shard_map/pallas_call | solution.py:306
  170.1 153.3 %all_to_all.20.fields_ref = bf16[32,12,8,1024]{3,2,1,0:T(8,128)(2,1)S(1)} all-to-all(bf16[32,12,8,1024]{3,2,1,0:T(8,128)(2,1)} %shard_map.80), channel_id=1, replica_groups=mesh['member'=32,'patch'=4,'level'=2] {'member'}, dimensions={0} | all-to-all | bytes 12582912 | tf_op jit(solution)/shard_map/all_to_all | solution.py:25
  323.4 3.9 %shard_map.81 = bf16[8,12,32,1024]{3,2,1,0:T(8,128)(2,1)} custom-call(bf16[32,12,8,1024]{3,2,1,0:T(8,128)(2,1)S(1)} %all_to_all.20.fields_ref), custom_call_target="tpu_custom_call" | custom-call | bytes 12582912 | tf_op jit(solution)/shard_map/pallas_call | solution.py:209
  (77 shorter events, 26.9 us)
Async XLA Ops:
  0.0 32.4 %copy-start.19 = (f32[1,12]{1,0:T(1,128)S(1)}, f32[1,12]{1,0:T(1,128)}, u32[]{:S(2)}) copy-start(f32[1,12]{1,0:T(1,128)} %param.12) | copy-start | bytes 148
  1.5 30.8 %all-to-all-start = ((f32[32,6,128]{2,1,0:T(8,128)}), f32[32,6,128]{2,1,0:T(8,128)S(1)}, u32[]{:S(2)}, u32[]{:S(2)}) async-start(f32[32,6,128]{2,1,0:T(8,128)} %shard_map.74), calls=%async_computation | async-start | bytes 262144 | tf_op jit(solution)/shard_map/all_to_all | solution.py:25
  19.2 29.3 %collective-permute-start = (bf16[4,6,8,1024]{3,2,1,0:T(8,128)(2,1)}, bf16[4,6,8,1024]{3,2,1,0:T(8,128)(2,1)S(1)}, u32[]{:S(2)}, u32[]{:S(2)}) collective-permute-start(bf16[4,6,8,1024]{3,2,1,0:T(8,128)(2,1)} %get-tuple-element.31), channel_id=1, source_target_pairs={{0,8},{8,16},{16,24},{24,32},{32,40},{40,48},{48,56},{56,0},{64,72... | collective-permute-start | bytes 1179656 | tf_op jit(solution)/shard_map/ppermute | solution.py:40
  21.0 27.5 %collective-permute-start.1 = (bf16[4,6,8,1024]{3,2,1,0:T(8,128)(2,1)}, bf16[4,6,8,1024]{3,2,1,0:T(8,128)(2,1)S(1)}, u32[]{:S(2)}, u32[]{:S(2)}) collective-permute-start(bf16[4,6,8,1024]{3,2,1,0:T(8,128)(2,1)} %get-tuple-element.32), channel_id=1, source_target_pairs={{0,56},{8,0},{16,8},{24,16},{32,24},{40,32},{48,40},{56,48},{64,12... | collective-permute-start | bytes 1179656 | tf_op jit(solution)/shard_map/ppermute | solution.py:40
  22.5 40.9 %collective-permute-start.2 = (bf16[4,6,8,1024]{3,2,1,0:T(8,128)(2,1)}, bf16[4,6,8,1024]{3,2,1,0:T(8,128)(2,1)S(1)}, u32[]{:S(2)}, u32[]{:S(2)}) collective-permute-start(bf16[4,6,8,1024]{3,2,1,0:T(8,128)(2,1)} %get-tuple-element.34), channel_id=1, source_target_pairs={{0,16},{8,24},{16,32},{24,40},{32,48},{40,56},{48,0},{56,8},{64,80... | collective-permute-start | bytes 1179656 | tf_op jit(solution)/shard_map/ppermute | solution.py:40
  23.9 39.4 %collective-permute-start.3 = (bf16[4,6,8,1024]{3,2,1,0:T(8,128)(2,1)}, bf16[4,6,8,1024]{3,2,1,0:T(8,128)(2,1)S(1)}, u32[]{:S(2)}, u32[]{:S(2)}) collective-permute-start(bf16[4,6,8,1024]{3,2,1,0:T(8,128)(2,1)} %get-tuple-element.35), channel_id=1, source_target_pairs={{0,32},{8,40},{16,48},{24,56},{32,0},{40,8},{48,16},{56,24},{64,96... | collective-permute-start | bytes 1179656 | tf_op jit(solution)/shard_map/ppermute | solution.py:40
  28.2 42.7 %collective-permute-start.4 = (bf16[4,6,8,1024]{3,2,1,0:T(8,128)(2,1)}, bf16[4,6,8,1024]{3,2,1,0:T(8,128)(2,1)S(1)}, u32[]{:S(2)}, u32[]{:S(2)}) collective-permute-start(bf16[4,6,8,1024]{3,2,1,0:T(8,128)(2,1)} %get-tuple-element.36), channel_id=1, source_target_pairs={{0,48},{8,56},{16,0},{24,8},{32,16},{40,24},{48,32},{56,40},{64,11... | collective-permute-start | bytes 1179656 | tf_op jit(solution)/shard_map/ppermute | solution.py:40
  48.5 29.3 %copy-start = (bf16[4,6,8,1024]{3,2,1,0:T(8,128)(2,1)}, bf16[4,6,8,1024]{3,2,1,0:T(8,128)(2,1)S(1)}, u32[]{:S(2)}) copy-start(bf16[4,6,8,1024]{3,2,1,0:T(8,128)(2,1)S(1)} %collective-permute-done.refs_1_) | copy-start | bytes 1179652
  48.5 29.2 %copy-start.1 = (bf16[4,6,8,1024]{3,2,1,0:T(8,128)(2,1)}, bf16[4,6,8,1024]{3,2,1,0:T(8,128)(2,1)S(1)}, u32[]{:S(2)}) copy-start(bf16[4,6,8,1024]{3,2,1,0:T(8,128)(2,1)S(1)} %collective-permute-done.1.refs_7_) | copy-start | bytes 1179652
  48.6 29.2 %all-to-all-start.1 = ((bf16[32,8,384]{2,1,0:T(8,128)(2,1)}), bf16[32,8,384]{2,1,0:T(8,128)(2,1)S(1)}, u32[]{:S(2)}, u32[]{:S(2)}) async-start(bf16[32,8,384]{2,1,0:T(8,128)(2,1)} %maximum_bitcast_fusion), calls=%async_computation.1 | async-start | bytes 393216 | tf_op jit(solution)/shard_map/all_to_all | solution.py:25
  54.8 43.8 %collective-permute-start.5 = (bf16[4,6,8,1024]{3,2,1,0:T(8,128)(2,1)}, bf16[4,6,8,1024]{3,2,1,0:T(8,128)(2,1)}, u32[]{:S(2)}, u32[]{:S(2)}) collective-permute-start(bf16[4,6,8,1024]{3,2,1,0:T(8,128)(2,1)} %get-tuple-element.38), channel_id=1, source_target_pairs={{0,24},{8,32},{16,40},{24,48},{32,56},{40,0},{48,8},{56,16},{64,88... | collective-permute-start | bytes 1179656 | tf_op jit(solution)/shard_map/ppermute | solution.py:40
  58.4 40.6 %collective-permute-start.6 = (bf16[4,6,8,1024]{3,2,1,0:T(8,128)(2,1)}, bf16[4,6,8,1024]{3,2,1,0:T(8,128)(2,1)}, u32[]{:S(2)}, u32[]{:S(2)}) collective-permute-start(bf16[4,6,8,1024]{3,2,1,0:T(8,128)(2,1)} %get-tuple-element.39), channel_id=1, source_target_pairs={{0,40},{8,48},{16,56},{24,0},{32,8},{40,16},{48,24},{56,32},{64,10... | collective-permute-start | bytes 1179656 | tf_op jit(solution)/shard_map/ppermute | solution.py:40
  63.3 25.7 %copy-start.2 = (bf16[4,6,8,1024]{3,2,1,0:T(8,128)(2,1)}, bf16[4,6,8,1024]{3,2,1,0:T(8,128)(2,1)S(1)}, u32[]{:S(2)}) copy-start(bf16[4,6,8,1024]{3,2,1,0:T(8,128)(2,1)S(1)} %collective-permute-done.2.refs_2_) | copy-start | bytes 1179652
  77.8 87.6 %all-to-all-start.2 = ((bf16[32,6,8,1024]{3,2,1,0:T(8,128)(2,1)}), bf16[32,6,8,1024]{3,2,1,0:T(8,128)(2,1)}, u32[]{:S(2)}, u32[]{:S(2)}) async-start(bf16[32,6,8,1024]{3,2,1,0:T(8,128)(2,1)} %shard_map.73), calls=%async_computation.2 | async-start | bytes 6291456 | tf_op jit(solution)/shard_map/all_to_all | solution.py:25
  103.1 39.9 %collective-permute-start.14 = (bf16[8,6,8,1024]{3,2,1,0:T(8,128)(2,1)}, bf16[8,6,8,1024]{3,2,1,0:T(8,128)(2,1)S(1)}, u32[]{:S(2)}, u32[]{:S(2)}) collective-permute-start(bf16[8,6,8,1024]{3,2,1,0:T(8,128)(2,1)} %get-tuple-element.52), channel_id=1, source_target_pairs={{0,64},{8,72},{16,80},{24,88},{32,96},{40,104},{48,112},{56,120},{... | collective-permute-start | bytes 2359304 | tf_op jit(solution)/shard_map/ppermute | solution.py:40
  104.6 54.3 %collective-permute-start.15 = (bf16[8,6,8,1024]{3,2,1,0:T(8,128)(2,1)}, bf16[8,6,8,1024]{3,2,1,0:T(8,128)(2,1)S(1)}, u32[]{:S(2)}, u32[]{:S(2)}) collective-permute-start(bf16[8,6,8,1024]{3,2,1,0:T(8,128)(2,1)} %get-tuple-element.53), channel_id=1, source_target_pairs={{0,128},{8,136},{16,144},{24,152},{32,160},{40,168},{48,176},{56,1... | collective-permute-start | bytes 2359304 | tf_op jit(solution)/shard_map/ppermute | solution.py:40
  107.3 51.9 %collective-permute-start.16 = (bf16[8,6,8,1024]{3,2,1,0:T(8,128)(2,1)}, bf16[8,6,8,1024]{3,2,1,0:T(8,128)(2,1)S(1)}, u32[]{:S(2)}, u32[]{:S(2)}) collective-permute-start(bf16[8,6,8,1024]{3,2,1,0:T(8,128)(2,1)} %get-tuple-element.54), channel_id=1, source_target_pairs={{0,192},{8,200},{16,208},{24,216},{32,224},{40,232},{48,240},{56,2... | collective-permute-start | bytes 2359304 | tf_op jit(solution)/shard_map/ppermute | solution.py:40
  108.7 13.8 %collective-permute-start.10 = (bf16[256,384]{1,0:T(8,128)(2,1)}, bf16[256,384]{1,0:T(8,128)(2,1)S(1)}, u32[]{:S(2)}, u32[]{:S(2)}) collective-permute-start(bf16[256,384]{1,0:T(8,128)(2,1)} %shard_map.76.refs_1_), channel_id=1, source_target_pairs={{0,1},{1,0},{2,3},{3,2},{4,5},{5,4},{6,7},{7,6},{8,9},{9,8},{10,11... | collective-permute-start | bytes 589832 | tf_op jit(solution)/shard_map/ppermute | solution.py:44
  108.8 4.1 %collective-permute-start.13 = (f32[3,4,128]{2,1,0:T(4,128)S(1)}, f32[3,4,128]{2,1,0:T(4,128)S(1)}, u32[]{:S(2)}, u32[]{:S(2)}) collective-permute-start(f32[3,4,128]{2,1,0:T(4,128)S(1)} %pad_dynamic-slice_fusion.refs_7_), channel_id=1, source_target_pairs={{2,0},{4,2},{6,4},{3,1},{5,3},{7,5},{10,8},{12,10},{14,12},{11,9},... | collective-permute-start | bytes 18440 | tf_op jit(solution)/shard_map/ppermute | solution.py:31
  112.9 5.8 %collective-permute-start.12 = (f32[3,4,128]{2,1,0:T(4,128)S(1)}, f32[3,4,128]{2,1,0:T(4,128)S(1)}, u32[]{:S(2)}, u32[]{:S(2)}) collective-permute-start(f32[3,4,128]{2,1,0:T(4,128)S(1)} %pad_dynamic-slice_fusion.refs_7_), channel_id=1, source_target_pairs={{0,2},{2,4},{4,6},{1,3},{3,5},{5,7},{8,10},{10,12},{12,14},{9,11},... | collective-permute-start | bytes 18440 | tf_op jit(solution)/shard_map/ppermute | solution.py:30
  118.7 7.4 %collective-permute-start.8 = (bf16[256,384]{1,0:T(8,128)(2,1)}, bf16[256,384]{1,0:T(8,128)(2,1)S(1)}, u32[]{:S(2)}, u32[]{:S(2)}) collective-permute-start(bf16[256,384]{1,0:T(8,128)(2,1)} %shard_map.76.refs_1_), channel_id=1, source_target_pairs={{2,0},{4,2},{6,4},{3,1},{5,3},{7,5},{10,8},{12,10},{14,12},{11,9},... | collective-permute-start | bytes 589832 | tf_op jit(solution)/shard_map/ppermute | solution.py:31
  122.6 7.8 %collective-permute-start.7 = (bf16[256,384]{1,0:T(8,128)(2,1)}, bf16[256,384]{1,0:T(8,128)(2,1)S(1)}, u32[]{:S(2)}, u32[]{:S(2)}) collective-permute-start(bf16[256,384]{1,0:T(8,128)(2,1)} %shard_map.76.refs_1_), channel_id=1, source_target_pairs={{0,2},{2,4},{4,6},{1,3},{3,5},{5,7},{8,10},{10,12},{12,14},{9,11},... | collective-permute-start | bytes 589832 | tf_op jit(solution)/shard_map/ppermute | solution.py:30
  126.1 4.3 %collective-permute-start.11 = (bf16[256,384]{1,0:T(8,128)(2,1)S(1)}, bf16[256,384]{1,0:T(8,128)(2,1)S(1)}, u32[]{:S(2)}, u32[]{:S(2)}) collective-permute-start(bf16[256,384]{1,0:T(8,128)(2,1)S(1)} %collective-permute-done.8.refs_2_), channel_id=1, source_target_pairs={{0,1},{1,0},{2,3},{3,2},{4,5},{5,4},{6,7},{7,6},{8,9},{9,8},{10,11... | collective-permute-start | bytes 589832 | tf_op jit(solution)/shard_map/ppermute | solution.py:44
  130.4 1.4 collective-permute-start.9
  (16 other events, 167.3 us)

commit v5 on v4

--- a/solution.py
+++ b/solution.py
@@ -13,7 +13,7 @@
 SWEEPS = 6
 FIRST = 6
 STEP = 3
-PAIR = 2
+PAIR = 3
 DEPTHS = 8
 TURNS = 4
 

time: 328 us -> 325 us (level)
  no operation moved by 1% of the time
where the time goes in v5:
time: 325 us
  blocking collectives  158 us (49%)
  starting transfers between devices  60.2 us (19%)
  waiting for transfers between devices  53.8 us (17%)
  Pallas kernels  37.8 us (12%)
  matrix products  10.7 us (3%)
    all_to_all x1, blocking collectives, exchange(): lax.all_to_all(cells, 'member', split_axis=0, concat_axis=0, tiled=True)  154 us
    ppermute x10, waiting for transfers between devices, shifted(): return lax.ppermute(cells, 'member', pairs)  33.2 us
    all_to_all x3, starting transfers between devices, exchange(): lax.all_to_all(cells, 'member', split_axis=0, concat_axis=0, tiled=True)  27.2 us
    ppermute x10, starting transfers between devices, shifted(): return lax.ppermute(cells, 'member', pairs)  23.8 us
    dot_general x1, matrix products, observe(): jnp.einsum('kpvq,pqo->kpvo', shaped_fields, column_hot, preferred_element...  10.7 us
    pallas_call x1, Pallas kernels, weights_for(): pl.pallas_call(weights_kernel, in_specs=[smem, smem] + [vmem] * 9, out_sp...  10.5 us
    ppermute x2, waiting for transfers between devices, row_halo(): above = lax.ppermute(cells, 'patch', [(i, i + 1) for i in range(count - 1)])  8.66 us
    pallas_call x2, Pallas kernels, turned(): pl.pallas_call(turn_kernel, grid=(levels // STEP,), in_specs=[pl.BlockSpe...  7.36 us
  transfers between devices with their start and end apart: 20, of which 11 were waited for; matrix products, arithmetic and copies ran while one was open for 4% of the time, Pallas kernels for 9%

profile of v5, /device:TPU:6, one launch (start us, length us, event | category | flops | bytes accessed | tf_op | source)
XLA Modules:
  0.0 324.6 jit_solution(11775369311815309084)
XLA Ops:
  1.5 11.5 %all-to-all-start = ((f32[32,6,128]{2,1,0:T(8,128)}), f32[32,6,128]{2,1,0:T(8,128)S(1)}, u32[]{:S(2)}, u32[]{:S(2)}) async-start(f32[32,6,128]{2,1,0:T(8,128)} %shard_map.74), calls=%async_computation | async-start | bytes 262144 | tf_op jit(solution)/shard_map/all_to_all | solution.py:25
  13.6 4.4 %shard_map.75 = (bf16[4,6,8,1024]{3,2,1,0:T(8,128)(2,1)}, bf16[4,6,8,1024]{3,2,1,0:T(8,128)(2,1)}, bf16[4,6,8,1024]{3,2,1,0:T(8,128)(2,1)}, bf16[4,6,8,1024]{3,2...) custom-call(s32[3]{0:T(128)} %pad_add_fusion.place_ref, ...), custom_call_target="tpu_custom_call" | custom-call | bytes 6291456 | tf_op jit(solution)/shard_map/pallas_call | solution.py:159
  22.7 4.2 %collective-permute-start.3 = (bf16[4,6,8,1024]{3,2,1,0:T(8,128)(2,1)}, bf16[4,6,8,1024]{3,2,1,0:T(8,128)(2,1)S(1)}, u32[]{:S(2)}, u32[]{:S(2)}) collective-permute-start(bf16[4,6,8,1024]{3,2,1,0:T(8,128)(2,1)} %get-tuple-element.35), channel_id=1, source_target_pairs={{0,32},{8,40},{16,48},{24,56},{32,0},{40,8},{48,16},{56,24},{64,96... | collective-permute-start | bytes 1179656 | tf_op jit(solution)/shard_map/ppermute | solution.py:40
  26.9 4.1 %collective-permute-start.4 = (bf16[4,6,8,1024]{3,2,1,0:T(8,128)(2,1)}, bf16[4,6,8,1024]{3,2,1,0:T(8,128)(2,1)S(1)}, u32[]{:S(2)}, u32[]{:S(2)}) collective-permute-start(bf16[4,6,8,1024]{3,2,1,0:T(8,128)(2,1)} %get-tuple-element.36), channel_id=1, source_target_pairs={{0,48},{8,56},{16,0},{24,8},{32,16},{40,24},{48,32},{56,40},{64,11... | collective-permute-start | bytes 1179656 | tf_op jit(solution)/shard_map/ppermute | solution.py:40
  31.7 10.7 %fusion.5 = f32[8,32,256]{2,0,1:T(8,128)S(1)} fusion(bf16[8,32,12,1024]{3,1,2,0:T(8,128)(2,1)} %bitcast.59, s32[32,256]{1,0:T(8,128)S(1)} %get-tuple-element.60, f32[32,12,256]{2,1,0:T(8,128)S(1)} %fusion.10), kind=kOutput, calls=%fused_computation.6 | convolution fusion | flops 1620508672 | bytes 6979584 | tf_op jit(solution)/shard_map/kpvq,pqo->kpvo/dot_general | solution.py:331
  42.4 4.2 %all-reduce.3 = bf16[8,32,256]{2,0,1:T(8,128)(2,1)S(1)} all-reduce(f32[8,32,256]{2,0,1:T(8,128)S(1)} %fusion.5), channel_id=1, replica_groups=mesh['member'=32,'patch'=4,'level'=2] {'level'}, use_global_device_ids=true, to_apply=%region_1.2 | all-reduce | flops 65536 | bytes 393216 | tf_op jit(solution)/shard_map/psum | solution.py:367
  47.3 6.2 %all-to-all-start.1 = ((bf16[32,8,384]{2,1,0:T(8,128)(2,1)}), bf16[32,8,384]{2,1,0:T(8,128)(2,1)S(1)}, u32[]{:S(2)}, u32[]{:S(2)}) async-start(bf16[32,8,384]{2,1,0:T(8,128)(2,1)} %maximum_bitcast_fusion), calls=%async_computation.1 | async-start | bytes 393216 | tf_op jit(solution)/shard_map/all_to_all | solution.py:25
  53.5 3.7 %collective-permute-start.5 = (bf16[4,6,8,1024]{3,2,1,0:T(8,128)(2,1)}, bf16[4,6,8,1024]{3,2,1,0:T(8,128)(2,1)}, u32[]{:S(2)}, u32[]{:S(2)}) collective-permute-start(bf16[4,6,8,1024]{3,2,1,0:T(8,128)(2,1)} %get-tuple-element.38), channel_id=1, source_target_pairs={{0,24},{8,32},{16,40},{24,48},{32,56},{40,0},{48,8},{56,16},{64,88... | collective-permute-start | bytes 1179656 | tf_op jit(solution)/shard_map/ppermute | solution.py:40
  58.6 3.4 %shard_map.73 = bf16[32,6,8,1024]{3,2,1,0:T(8,128)(2,1)} custom-call(bf16[8,12,32,1024]{3,2,1,0:T(8,128)(2,1)} %bitcast.60), custom_call_target="tpu_custom_call" | custom-call | bytes 12582912 | tf_op jit(solution)/shard_map/pallas_call | solution.py:209
  62.1 7.5 %collective-permute-done.4.refs_6_ = bf16[4,6,8,1024]{3,2,1,0:T(8,128)(2,1)S(1)} collective-permute-done((bf16[4,6,8,1024]{3,2,1,0:T(8,128)(2,1)}, bf16[4,6,8,1024]{3,2,1,0:T(8,128)(2,1)S(1)}, u32[]{:S(2)}, u32[]{:S(2)}) %collective-permute-start.4) | collective-permute-done | bytes 393248 | tf_op jit(solution)/shard_map/ppermute | solution.py:40
  69.7 6.9 %all-to-all-done.1 = bf16[32,8,384]{2,1,0:T(8,128)(2,1)S(1)} async-done(((bf16[32,8,384]{2,1,0:T(8,128)(2,1)}), bf16[32,8,384]{2,1,0:T(8,128)(2,1)S(1)}, u32[]{:S(2)}, u32[]{:S(2)}) %all-to-all-start.1) | async-done | bytes 196640 | tf_op jit(solution)/shard_map/all_to_all | solution.py:25
  76.6 9.5 %all-to-all-start.2 = ((bf16[32,6,8,1024]{3,2,1,0:T(8,128)(2,1)}), bf16[32,6,8,1024]{3,2,1,0:T(8,128)(2,1)}, u32[]{:S(2)}, u32[]{:S(2)}) async-start(bf16[32,6,8,1024]{3,2,1,0:T(8,128)(2,1)} %shard_map.73), calls=%async_computation.2 | async-start | bytes 6291456 | tf_op jit(solution)/shard_map/all_to_all | solution.py:25
  87.8 9.5 %collective-permute-done.5.refs_3_ = bf16[4,6,8,1024]{3,2,1,0:T(8,128)(2,1)} collective-permute-done((bf16[4,6,8,1024]{3,2,1,0:T(8,128)(2,1)}, bf16[4,6,8,1024]{3,2,1,0:T(8,128)(2,1)}, u32[]{:S(2)}, u32[]{:S(2)}) %collective-permute-start.5) | collective-permute-done | bytes 393248 | tf_op jit(solution)/shard_map/ppermute | solution.py:40
  97.8 3.1 shard_map.78
  106.5 2.7 collective-permute-start.13
  111.9 4.5 %collective-permute-done.12.refs_6_ = f32[3,4,128]{2,1,0:T(4,128)S(1)} collective-permute-done((f32[3,4,128]{2,1,0:T(4,128)S(1)}, f32[3,4,128]{2,1,0:T(4,128)S(1)}, u32[]{:S(2)}, u32[]{:S(2)}) %collective-permute-start.12) | collective-permute-done | bytes 6176 | tf_op jit(solution)/shard_map/ppermute | solution.py:30
  116.4 3.9 %collective-permute-start.8 = (bf16[256,384]{1,0:T(8,128)(2,1)}, bf16[256,384]{1,0:T(8,128)(2,1)S(1)}, u32[]{:S(2)}, u32[]{:S(2)}) collective-permute-start(bf16[256,384]{1,0:T(8,128)(2,1)} %shard_map.76.refs_1_), channel_id=1, source_target_pairs={{2,0},{4,2},{6,4},{3,1},{5,3},{7,5},{10,8},{12,10},{14,12},{11,9},... | collective-permute-start | bytes 589832 | tf_op jit(solution)/shard_map/ppermute | solution.py:31
  123.9 4.2 %collective-permute-done.7.refs_0_ = bf16[256,384]{1,0:T(8,128)(2,1)S(1)} collective-permute-done((bf16[256,384]{1,0:T(8,128)(2,1)}, bf16[256,384]{1,0:T(8,128)(2,1)S(1)}, u32[]{:S(2)}, u32[]{:S(2)}) %collective-permute-start.7) | collective-permute-done | bytes 196640 | tf_op jit(solution)/shard_map/ppermute | solution.py:30
  130.2 10.5 %shard_map.77 = (bf16[256,256]{1,0:T(8,128)(2,1)}, bf16[256,256]{1,0:T(8,128)(2,1)}) custom-call(s32[8]{0:T(128)} %bitcast.68, s32[3]{0:T(128)} %pad_add_fusion.place_ref, bf16[256,384]{1,0:T(8,128)(2,1)} %copy-done.13, bf16[256,384]{1,0:T(8,128)(2,1)} %shard_map.76.refs_1_, bf16[256,384]{1,0:T(8,128)(2,1)} %copy-done.12, bf16[256,384]{1,0:T(8,128)(2,1)} %copy-done.15, ...), custom_call_target="tpu_custom_call" | custom-call | bytes 1024 | tf_op jit(solution)/shard_map/pallas_call | solution.py:131
  140.7 15.5 %collective-permute-done.15.refs_9_ = bf16[8,6,8,1024]{3,2,1,0:T(8,128)(2,1)S(1)} collective-permute-done((bf16[8,6,8,1024]{3,2,1,0:T(8,128)(2,1)}, bf16[8,6,8,1024]{3,2,1,0:T(8,128)(2,1)S(1)}, u32[]{:S(2)}, u32[]{:S(2)}) %collective-permute-start.15) | collective-permute-done | bytes 786464 | tf_op jit(solution)/shard_map/ppermute | solution.py:40
  157.4 4.7 %shard_map.79._ = bf16[32,12,8,1024]{3,2,1,0:T(8,128)(2,1)} custom-call(bf16[256,256]{1,0:T(8,128)(2,1)} %get-tuple-element.43.weights_ref, bf16[4,6,8,1024]{3,2,1,0:T(8,128)(2,1)} %get-tuple-element.44.refs_0_, bf16[4,6,8,1024]{3,2,1,0:T(8,128)(2,1)} %copy-done, bf16[4,6,8,1024]{3,2,1,0:T(8,128)(2,1)} %copy-done.2, ...), custom_call_target="tpu_custom_call" | custom-call | flops 805306368 | bytes 6291456 | tf_op jit(solution)/shard_map/pallas_call | solution.py:281
  162.1 4.6 %shard_map.80 = bf16[32,12,8,1024]{3,2,1,0:T(8,128)(2,1)} custom-call(bf16[256,256]{1,0:T(8,128)(2,1)} %get-tuple-element.41.weights_ref, bf16[32,6,8,1024]{3,2,1,0:T(8,128)(2,1)} %all-to-all-done.2.fields_ref, bf16[32,12,8,1024]{3,2,1,0:T(8,128)(2,1)} %shard_map.79._), custom_call_target="tpu_custom_call", output_to_operand_aliasing={{}: (2, {})} | custom-call | flops 805306368 | bytes 6291456 | tf_op jit(solution)/shard_map/pallas_call | solution.py:306
  166.7 153.9 %all_to_all.20.fields_ref = bf16[32,12,8,1024]{3,2,1,0:T(8,128)(2,1)S(1)} all-to-all(bf16[32,12,8,1024]{3,2,1,0:T(8,128)(2,1)} %shard_map.80), channel_id=1, replica_groups=mesh['member'=32,'patch'=4,'level'=2] {'member'}, dimensions={0} | all-to-all | bytes 12582912 | tf_op jit(solution)/shard_map/all_to_all | solution.py:25
  320.7 3.9 %shard_map.81 = bf16[8,12,32,1024]{3,2,1,0:T(8,128)(2,1)} custom-call(bf16[32,12,8,1024]{3,2,1,0:T(8,128)(2,1)S(1)} %all_to_all.20.fields_ref), custom_call_target="tpu_custom_call" | custom-call | bytes 12582912 | tf_op jit(solution)/shard_map/pallas_call | solution.py:209
  (77 shorter events, 26.9 us)
Async XLA Ops:
  0.0 31.1 %copy-start.19 = (f32[1,12]{1,0:T(1,128)S(1)}, f32[1,12]{1,0:T(1,128)}, u32[]{:S(2)}) copy-start(f32[1,12]{1,0:T(1,128)} %param.12) | copy-start | bytes 148
  1.5 29.6 %all-to-all-start = ((f32[32,6,128]{2,1,0:T(8,128)}), f32[32,6,128]{2,1,0:T(8,128)S(1)}, u32[]{:S(2)}, u32[]{:S(2)}) async-start(f32[32,6,128]{2,1,0:T(8,128)} %shard_map.74), calls=%async_computation | async-start | bytes 262144 | tf_op jit(solution)/shard_map/all_to_all | solution.py:25
  18.0 29.3 %collective-permute-start = (bf16[4,6,8,1024]{3,2,1,0:T(8,128)(2,1)}, bf16[4,6,8,1024]{3,2,1,0:T(8,128)(2,1)S(1)}, u32[]{:S(2)}, u32[]{:S(2)}) collective-permute-start(bf16[4,6,8,1024]{3,2,1,0:T(8,128)(2,1)} %get-tuple-element.31), channel_id=1, source_target_pairs={{0,8},{8,16},{16,24},{24,32},{32,40},{40,48},{48,56},{56,0},{64,72... | collective-permute-start | bytes 1179656 | tf_op jit(solution)/shard_map/ppermute | solution.py:40
  19.8 27.5 %collective-permute-start.1 = (bf16[4,6,8,1024]{3,2,1,0:T(8,128)(2,1)}, bf16[4,6,8,1024]{3,2,1,0:T(8,128)(2,1)S(1)}, u32[]{:S(2)}, u32[]{:S(2)}) collective-permute-start(bf16[4,6,8,1024]{3,2,1,0:T(8,128)(2,1)} %get-tuple-element.32), channel_id=1, source_target_pairs={{0,56},{8,0},{16,8},{24,16},{32,24},{40,32},{48,40},{56,48},{64,12... | collective-permute-start | bytes 1179656 | tf_op jit(solution)/shard_map/ppermute | solution.py:40
  21.2 40.9 %collective-permute-start.2 = (bf16[4,6,8,1024]{3,2,1,0:T(8,128)(2,1)}, bf16[4,6,8,1024]{3,2,1,0:T(8,128)(2,1)S(1)}, u32[]{:S(2)}, u32[]{:S(2)}) collective-permute-start(bf16[4,6,8,1024]{3,2,1,0:T(8,128)(2,1)} %get-tuple-element.34), channel_id=1, source_target_pairs={{0,16},{8,24},{16,32},{24,40},{32,48},{40,56},{48,0},{56,8},{64,80... | collective-permute-start | bytes 1179656 | tf_op jit(solution)/shard_map/ppermute | solution.py:40
  22.7 39.4 %collective-permute-start.3 = (bf16[4,6,8,1024]{3,2,1,0:T(8,128)(2,1)}, bf16[4,6,8,1024]{3,2,1,0:T(8,128)(2,1)S(1)}, u32[]{:S(2)}, u32[]{:S(2)}) collective-permute-start(bf16[4,6,8,1024]{3,2,1,0:T(8,128)(2,1)} %get-tuple-element.35), channel_id=1, source_target_pairs={{0,32},{8,40},{16,48},{24,56},{32,0},{40,8},{48,16},{56,24},{64,96... | collective-permute-start | bytes 1179656 | tf_op jit(solution)/shard_map/ppermute | solution.py:40
  26.9 42.7 %collective-permute-start.4 = (bf16[4,6,8,1024]{3,2,1,0:T(8,128)(2,1)}, bf16[4,6,8,1024]{3,2,1,0:T(8,128)(2,1)S(1)}, u32[]{:S(2)}, u32[]{:S(2)}) collective-permute-start(bf16[4,6,8,1024]{3,2,1,0:T(8,128)(2,1)} %get-tuple-element.36), channel_id=1, source_target_pairs={{0,48},{8,56},{16,0},{24,8},{32,16},{40,24},{48,32},{56,40},{64,11... | collective-permute-start | bytes 1179656 | tf_op jit(solution)/shard_map/ppermute | solution.py:40
  47.3 29.3 %copy-start = (bf16[4,6,8,1024]{3,2,1,0:T(8,128)(2,1)}, bf16[4,6,8,1024]{3,2,1,0:T(8,128)(2,1)S(1)}, u32[]{:S(2)}) copy-start(bf16[4,6,8,1024]{3,2,1,0:T(8,128)(2,1)S(1)} %collective-permute-done.refs_1_) | copy-start | bytes 1179652
  47.3 29.3 %copy-start.1 = (bf16[4,6,8,1024]{3,2,1,0:T(8,128)(2,1)}, bf16[4,6,8,1024]{3,2,1,0:T(8,128)(2,1)S(1)}, u32[]{:S(2)}) copy-start(bf16[4,6,8,1024]{3,2,1,0:T(8,128)(2,1)S(1)} %collective-permute-done.1.refs_7_) | copy-start | bytes 1179652
  47.3 29.2 %all-to-all-start.1 = ((bf16[32,8,384]{2,1,0:T(8,128)(2,1)}), bf16[32,8,384]{2,1,0:T(8,128)(2,1)S(1)}, u32[]{:S(2)}, u32[]{:S(2)}) async-start(bf16[32,8,384]{2,1,0:T(8,128)(2,1)} %maximum_bitcast_fusion), calls=%async_computation.1 | async-start | bytes 393216 | tf_op jit(solution)/shard_map/all_to_all | solution.py:25
  53.5 43.8 %collective-permute-start.5 = (bf16[4,6,8,1024]{3,2,1,0:T(8,128)(2,1)}, bf16[4,6,8,1024]{3,2,1,0:T(8,128)(2,1)}, u32[]{:S(2)}, u32[]{:S(2)}) collective-permute-start(bf16[4,6,8,1024]{3,2,1,0:T(8,128)(2,1)} %get-tuple-element.38), channel_id=1, source_target_pairs={{0,24},{8,32},{16,40},{24,48},{32,56},{40,0},{48,8},{56,16},{64,88... | collective-permute-start | bytes 1179656 | tf_op jit(solution)/shard_map/ppermute | solution.py:40
  57.2 40.6 %collective-permute-start.6 = (bf16[4,6,8,1024]{3,2,1,0:T(8,128)(2,1)}, bf16[4,6,8,1024]{3,2,1,0:T(8,128)(2,1)}, u32[]{:S(2)}, u32[]{:S(2)}) collective-permute-start(bf16[4,6,8,1024]{3,2,1,0:T(8,128)(2,1)} %get-tuple-element.39), channel_id=1, source_target_pairs={{0,40},{8,48},{16,56},{24,0},{32,8},{40,16},{48,24},{56,32},{64,10... | collective-permute-start | bytes 1179656 | tf_op jit(solution)/shard_map/ppermute | solution.py:40
  62.1 25.7 %copy-start.2 = (bf16[4,6,8,1024]{3,2,1,0:T(8,128)(2,1)}, bf16[4,6,8,1024]{3,2,1,0:T(8,128)(2,1)S(1)}, u32[]{:S(2)}) copy-start(bf16[4,6,8,1024]{3,2,1,0:T(8,128)(2,1)S(1)} %collective-permute-done.2.refs_2_) | copy-start | bytes 1179652
  76.6 85.5 %all-to-all-start.2 = ((bf16[32,6,8,1024]{3,2,1,0:T(8,128)(2,1)}), bf16[32,6,8,1024]{3,2,1,0:T(8,128)(2,1)}, u32[]{:S(2)}, u32[]{:S(2)}) async-start(bf16[32,6,8,1024]{3,2,1,0:T(8,128)(2,1)} %shard_map.73), calls=%async_computation.2 | async-start | bytes 6291456 | tf_op jit(solution)/shard_map/all_to_all | solution.py:25
  100.8 39.9 %collective-permute-start.14 = (bf16[8,6,8,1024]{3,2,1,0:T(8,128)(2,1)}, bf16[8,6,8,1024]{3,2,1,0:T(8,128)(2,1)S(1)}, u32[]{:S(2)}, u32[]{:S(2)}) collective-permute-start(bf16[8,6,8,1024]{3,2,1,0:T(8,128)(2,1)} %get-tuple-element.52), channel_id=1, source_target_pairs={{0,64},{8,72},{16,80},{24,88},{32,96},{40,104},{48,112},{56,120},{... | collective-permute-start | bytes 2359304 | tf_op jit(solution)/shard_map/ppermute | solution.py:40
  102.3 53.9 %collective-permute-start.15 = (bf16[8,6,8,1024]{3,2,1,0:T(8,128)(2,1)}, bf16[8,6,8,1024]{3,2,1,0:T(8,128)(2,1)S(1)}, u32[]{:S(2)}, u32[]{:S(2)}) collective-permute-start(bf16[8,6,8,1024]{3,2,1,0:T(8,128)(2,1)} %get-tuple-element.53), channel_id=1, source_target_pairs={{0,128},{8,136},{16,144},{24,152},{32,160},{40,168},{48,176},{56,1... | collective-permute-start | bytes 2359304 | tf_op jit(solution)/shard_map/ppermute | solution.py:40
  105.0 51.4 %collective-permute-start.16 = (bf16[8,6,8,1024]{3,2,1,0:T(8,128)(2,1)}, bf16[8,6,8,1024]{3,2,1,0:T(8,128)(2,1)S(1)}, u32[]{:S(2)}, u32[]{:S(2)}) collective-permute-start(bf16[8,6,8,1024]{3,2,1,0:T(8,128)(2,1)} %get-tuple-element.54), channel_id=1, source_target_pairs={{0,192},{8,200},{16,208},{24,216},{32,224},{40,232},{48,240},{56,2... | collective-permute-start | bytes 2359304 | tf_op jit(solution)/shard_map/ppermute | solution.py:40
  106.5 13.8 %collective-permute-start.10 = (bf16[256,384]{1,0:T(8,128)(2,1)}, bf16[256,384]{1,0:T(8,128)(2,1)S(1)}, u32[]{:S(2)}, u32[]{:S(2)}) collective-permute-start(bf16[256,384]{1,0:T(8,128)(2,1)} %shard_map.76.refs_1_), channel_id=1, source_target_pairs={{0,1},{1,0},{2,3},{3,2},{4,5},{5,4},{6,7},{7,6},{8,9},{9,8},{10,11... | collective-permute-start | bytes 589832 | tf_op jit(solution)/shard_map/ppermute | solution.py:44
  106.5 4.1 %collective-permute-start.13 = (f32[3,4,128]{2,1,0:T(4,128)S(1)}, f32[3,4,128]{2,1,0:T(4,128)S(1)}, u32[]{:S(2)}, u32[]{:S(2)}) collective-permute-start(f32[3,4,128]{2,1,0:T(4,128)S(1)} %pad_dynamic-slice_fusion.refs_7_), channel_id=1, source_target_pairs={{2,0},{4,2},{6,4},{3,1},{5,3},{7,5},{10,8},{12,10},{14,12},{11,9},... | collective-permute-start | bytes 18440 | tf_op jit(solution)/shard_map/ppermute | solution.py:31
  110.6 5.8 %collective-permute-start.12 = (f32[3,4,128]{2,1,0:T(4,128)S(1)}, f32[3,4,128]{2,1,0:T(4,128)S(1)}, u32[]{:S(2)}, u32[]{:S(2)}) collective-permute-start(f32[3,4,128]{2,1,0:T(4,128)S(1)} %pad_dynamic-slice_fusion.refs_7_), channel_id=1, source_target_pairs={{0,2},{2,4},{4,6},{1,3},{3,5},{5,7},{8,10},{10,12},{12,14},{9,11},... | collective-permute-start | bytes 18440 | tf_op jit(solution)/shard_map/ppermute | solution.py:30
  116.4 7.5 %collective-permute-start.8 = (bf16[256,384]{1,0:T(8,128)(2,1)}, bf16[256,384]{1,0:T(8,128)(2,1)S(1)}, u32[]{:S(2)}, u32[]{:S(2)}) collective-permute-start(bf16[256,384]{1,0:T(8,128)(2,1)} %shard_map.76.refs_1_), channel_id=1, source_target_pairs={{2,0},{4,2},{6,4},{3,1},{5,3},{7,5},{10,8},{12,10},{14,12},{11,9},... | collective-permute-start | bytes 589832 | tf_op jit(solution)/shard_map/ppermute | solution.py:31
  120.3 7.8 %collective-permute-start.7 = (bf16[256,384]{1,0:T(8,128)(2,1)}, bf16[256,384]{1,0:T(8,128)(2,1)S(1)}, u32[]{:S(2)}, u32[]{:S(2)}) collective-permute-start(bf16[256,384]{1,0:T(8,128)(2,1)} %shard_map.76.refs_1_), channel_id=1, source_target_pairs={{0,2},{2,4},{4,6},{1,3},{3,5},{5,7},{8,10},{10,12},{12,14},{9,11},... | collective-permute-start | bytes 589832 | tf_op jit(solution)/shard_map/ppermute | solution.py:30
  123.9 4.2 %collective-permute-start.11 = (bf16[256,384]{1,0:T(8,128)(2,1)S(1)}, bf16[256,384]{1,0:T(8,128)(2,1)S(1)}, u32[]{:S(2)}, u32[]{:S(2)}) collective-permute-start(bf16[256,384]{1,0:T(8,128)(2,1)S(1)} %collective-permute-done.8.refs_2_), channel_id=1, source_target_pairs={{0,1},{1,0},{2,3},{3,2},{4,5},{5,4},{6,7},{7,6},{8,9},{9,8},{10,11... | collective-permute-start | bytes 589832 | tf_op jit(solution)/shard_map/ppermute | solution.py:44
  128.1 1.4 collective-permute-start.9
  (16 other events, 165.7 us)
